TPU v7x, 128 devices: a whole 4x4x4 slice. The times are simulated.
128 devices in a mesh: ctx: 16 (over x_lo, y, core), head: 8 (over z, x_hi).
Axes of the slice: x: 4 (x_hi: 2, x_lo: 2; x = x_hi * 2 + x_lo), y: 4, z: 4, core: 2. Of those that a mesh axis runs over, the one named last changes fastest.
Arguments:
- queries: bfloat16 [1024, 16384], P('ctx', 'head'), may hold values from -8 to 8, as said below
- key_cache: bfloat16 [16384, 1024], P('ctx', 'head'), may hold values from -8 to 8, as said below
- value_cache: bfloat16 [16384, 1024], P('ctx', 'head'), may hold values from -5 to 5
- out_weight: bfloat16 [16384, 16384], P('head', 'ctx'), may hold values from -0.046875 to 0.046875
Outputs:
- projected: bfloat16 [1024, 16384], P('head', 'ctx')
Inputs may be any that keep to these rules, and one draw needn't show every extreme that they name: `queries`: entries of order one. `key_cache`: entries of order one.
All inputs are finite; a program needn't handle non-finite values.
Results may differ from a plain program's by a relative error of at most 0.012.
Values may be sent and summed in bfloat16 or wider, within the bound.
A program may use at most 320 MiB of HBM per device.

v0:
```python
import math

import jax
import jax.numpy as jnp
from jax import lax
from jax.sharding import PartitionSpec as P

HD = 128
CACHE_RUN = 64


NEG = -1e30


def passed_along(value, axis, steps):
    count = lax.axis_size(axis)
    pairs = [(source, (source + steps) % count) for source in range(count)]
    return lax.ppermute(value, axis, pairs)


def positions_of(row_ids, per_device, devices, run_len):
    device = row_ids // per_device
    within = row_ids % per_device
    return (within // run_len * devices + device) * run_len + within % run_len


def attend(query_block, query_pos, key_block, value_block, key_pos):
    tok_count = query_block.shape[0]
    kv_local = key_block.shape[1] // HD
    heads_local = query_block.shape[1] // HD
    group_size = heads_local // kv_local
    grouped = query_block.reshape(tok_count, kv_local, group_size, HD)
    key_view = key_block.reshape(-1, kv_local, HD)
    value_view = value_block.reshape(-1, kv_local, HD)
    scores = jnp.einsum("tkgd,ckd->tkgc", grouped, key_view, preferred_element_type=jnp.float32) * (
        1.0 / math.sqrt(HD)
    )
    visible = key_pos[None, None, None, :] <= query_pos[:, None, None, None]
    scores = jnp.where(visible, scores, NEG)
    row_max = jnp.max(scores, axis=-1)
    weights = jnp.where(visible, jnp.exp(scores - row_max[..., None]), 0.0)
    weight_sum = jnp.sum(weights, axis=-1)
    summed = jnp.einsum(
        "tkgc,ckd->tkgd",
        weights.astype(jnp.bfloat16),
        value_view,
        preferred_element_type=jnp.float32,
    )
    return (
        summed.reshape(tok_count, heads_local, HD),
        row_max.reshape(tok_count, heads_local),
        weight_sum.reshape(tok_count, heads_local),
    )


def combine(earlier, later):
    summed_a, maxed_a, totals_a = earlier
    summed_b, maxed_b, totals_b = later
    new_max = jnp.maximum(maxed_a, maxed_b)
    scale_a = jnp.exp(maxed_a - new_max)
    scale_b = jnp.exp(maxed_b - new_max)
    return (
        summed_a * scale_a[..., None] + summed_b * scale_b[..., None],
        new_max,
        totals_a * scale_a + totals_b * scale_b,
    )


def finish(state):
    summed, maxed, totals = state
    return (summed / totals[..., None]).reshape(summed.shape[0], -1).astype(jnp.bfloat16)


def empty_state(tok_count, heads_local):
    return (
        jnp.zeros((tok_count, heads_local, HD), jnp.float32),
        jnp.full((tok_count, heads_local), NEG, jnp.float32),
        jnp.zeros((tok_count, heads_local), jnp.float32),
    )


def body(queries, key_cache, value_cache, out_weight):
    tok_count, width = queries.shape
    heads_local = width // HD
    per_device = key_cache.shape[0]
    devices = lax.axis_size("ctx")
    my_index = lax.axis_index("ctx")
    turn = tok_count * devices
    turn_start = per_device * devices - turn
    local_rows = my_index * per_device + jnp.arange(per_device, dtype=jnp.int32)
    local_pos = positions_of(local_rows, per_device, devices, CACHE_RUN)

    def query_pos(owner):
        return turn_start + owner * tok_count + jnp.arange(tok_count, dtype=jnp.int32)

    def visit(step, carry):
        block = carry[0]
        owner = (my_index - step) % devices
        state = combine(
            carry[1:], attend(block, query_pos(owner), key_cache, value_cache, local_pos)
        )
        block = passed_along(block, "ctx", 1)
        state = passed_along((state[0], state[1], state[2]), "ctx", 1)
        return (block,) + tuple(state)

    start_state = (queries,) + empty_state(tok_count, heads_local)
    final = lax.fori_loop(0, devices, visit, start_state)
    attended = finish(final[1:])
    terms = jnp.dot(
        lax.all_gather(attended, "ctx", axis=0, tiled=True),
        out_weight,
        preferred_element_type=jnp.float32,
    )
    return lax.psum_scatter(terms, "head", scatter_dimension=0, tiled=True).astype(jnp.bfloat16)


def solution(mesh):
    in_specs = (P("ctx", "head"), P("ctx", "head"), P("ctx", "head"), P("head", "ctx"))
    out_specs = P("head", "ctx")
    return jax.shard_map(body, mesh=mesh, in_specs=in_specs, out_specs=out_specs, check_vma=False)
```

profile of v0, /device:TPU:0, one launch (start us, length us, event | category | flops | bytes accessed | tf_op | source)
XLA Modules:
  0.0 452.6 jit_solution(5590934774815793028)
XLA Ops:
  7.5 303.2 %while.22 = (s32[]{:T(128)}, bf16[64,2048]{1,0:T(8,128)(2,1)S(1)}, f32[64,16,128]{2,1,0:T(8,128)S(1)}, f32[64,16]{0,1:T(8,128)S(1)}, f32[64,16]{0,1:T(8,128)S(1)...) while((s32[]{:T(128)}, bf16[64,2048]{1,0:T(8,128)(2,1)S(1)}, ...), condition=%wide.region_3.4_spmd.clone, body=%wide.region_0.3_spmd.clone.sunk | while | flops 551009344 | bytes 20562912 | solution.py:107
  7.8 1.9 fusion.47
  16.3 10.1 %collective-permute-done.2 = f32[64,16]{0,1:T(8,128)S(1)} collective-permute-done((f32[64,16]{0,1:T(8,128)S(1)}, f32[64,16]{0,1:T(8,128)S(1)}, u32[]{:S(2)}, u32[]{:S(2)}) %collective-permute-start.2) | collective-permute-done | bytes 4128 | tf_op jit(solution)/shard_map/while/body/eval_jaxpr/ppermute | solution.py:18
  26.7 1.9 fusion.47
  33.1 12.3 %collective-permute-done.2 = f32[64,16]{0,1:T(8,128)S(1)} collective-permute-done((f32[64,16]{0,1:T(8,128)S(1)}, f32[64,16]{0,1:T(8,128)S(1)}, u32[]{:S(2)}, u32[]{:S(2)}) %collective-permute-start.2) | collective-permute-done | bytes 4128 | tf_op jit(solution)/shard_map/while/body/eval_jaxpr/ppermute | solution.py:18
  51.0 13.3 %collective-permute-done.2 = f32[64,16]{0,1:T(8,128)S(1)} collective-permute-done((f32[64,16]{0,1:T(8,128)S(1)}, f32[64,16]{0,1:T(8,128)S(1)}, u32[]{:S(2)}, u32[]{:S(2)}) %collective-permute-start.2) | collective-permute-done | bytes 4128 | tf_op jit(solution)/shard_map/while/body/eval_jaxpr/ppermute | solution.py:18
  64.6 1.9 fusion.47
  69.9 13.3 %collective-permute-done.2 = f32[64,16]{0,1:T(8,128)S(1)} collective-permute-done((f32[64,16]{0,1:T(8,128)S(1)}, f32[64,16]{0,1:T(8,128)S(1)}, u32[]{:S(2)}, u32[]{:S(2)}) %collective-permute-start.2) | collective-permute-done | bytes 4128 | tf_op jit(solution)/shard_map/while/body/eval_jaxpr/ppermute | solution.py:18
  83.5 1.9 fusion.47
  88.9 13.3 %collective-permute-done.2 = f32[64,16]{0,1:T(8,128)S(1)} collective-permute-done((f32[64,16]{0,1:T(8,128)S(1)}, f32[64,16]{0,1:T(8,128)S(1)}, u32[]{:S(2)}, u32[]{:S(2)}) %collective-permute-start.2) | collective-permute-done | bytes 4128 | tf_op jit(solution)/shard_map/while/body/eval_jaxpr/ppermute | solution.py:18
  107.8 13.3 %collective-permute-done.2 = f32[64,16]{0,1:T(8,128)S(1)} collective-permute-done((f32[64,16]{0,1:T(8,128)S(1)}, f32[64,16]{0,1:T(8,128)S(1)}, u32[]{:S(2)}, u32[]{:S(2)}) %collective-permute-start.2) | collective-permute-done | bytes 4128 | tf_op jit(solution)/shard_map/while/body/eval_jaxpr/ppermute | solution.py:18
  126.8 13.3 %collective-permute-done.2 = f32[64,16]{0,1:T(8,128)S(1)} collective-permute-done((f32[64,16]{0,1:T(8,128)S(1)}, f32[64,16]{0,1:T(8,128)S(1)}, u32[]{:S(2)}, u32[]{:S(2)}) %collective-permute-start.2) | collective-permute-done | bytes 4128 | tf_op jit(solution)/shard_map/while/body/eval_jaxpr/ppermute | solution.py:18
  145.7 13.3 %collective-permute-done.2 = f32[64,16]{0,1:T(8,128)S(1)} collective-permute-done((f32[64,16]{0,1:T(8,128)S(1)}, f32[64,16]{0,1:T(8,128)S(1)}, u32[]{:S(2)}, u32[]{:S(2)}) %collective-permute-start.2) | collective-permute-done | bytes 4128 | tf_op jit(solution)/shard_map/while/body/eval_jaxpr/ppermute | solution.py:18
  164.7 13.3 %collective-permute-done.2 = f32[64,16]{0,1:T(8,128)S(1)} collective-permute-done((f32[64,16]{0,1:T(8,128)S(1)}, f32[64,16]{0,1:T(8,128)S(1)}, u32[]{:S(2)}, u32[]{:S(2)}) %collective-permute-start.2) | collective-permute-done | bytes 4128 | tf_op jit(solution)/shard_map/while/body/eval_jaxpr/ppermute | solution.py:18
  183.6 13.3 %collective-permute-done.2 = f32[64,16]{0,1:T(8,128)S(1)} collective-permute-done((f32[64,16]{0,1:T(8,128)S(1)}, f32[64,16]{0,1:T(8,128)S(1)}, u32[]{:S(2)}, u32[]{:S(2)}) %collective-permute-start.2) | collective-permute-done | bytes 4128 | tf_op jit(solution)/shard_map/while/body/eval_jaxpr/ppermute | solution.py:18
  202.5 13.3 %collective-permute-done.2 = f32[64,16]{0,1:T(8,128)S(1)} collective-permute-done((f32[64,16]{0,1:T(8,128)S(1)}, f32[64,16]{0,1:T(8,128)S(1)}, u32[]{:S(2)}, u32[]{:S(2)}) %collective-permute-start.2) | collective-permute-done | bytes 4128 | tf_op jit(solution)/shard_map/while/body/eval_jaxpr/ppermute | solution.py:18
  221.5 13.3 %collective-permute-done.2 = f32[64,16]{0,1:T(8,128)S(1)} collective-permute-done((f32[64,16]{0,1:T(8,128)S(1)}, f32[64,16]{0,1:T(8,128)S(1)}, u32[]{:S(2)}, u32[]{:S(2)}) %collective-permute-start.2) | collective-permute-done | bytes 4128 | tf_op jit(solution)/shard_map/while/body/eval_jaxpr/ppermute | solution.py:18
  240.4 13.3 %collective-permute-done.2 = f32[64,16]{0,1:T(8,128)S(1)} collective-permute-done((f32[64,16]{0,1:T(8,128)S(1)}, f32[64,16]{0,1:T(8,128)S(1)}, u32[]{:S(2)}, u32[]{:S(2)}) %collective-permute-start.2) | collective-permute-done | bytes 4128 | tf_op jit(solution)/shard_map/while/body/eval_jaxpr/ppermute | solution.py:18
  259.4 13.3 %collective-permute-done.2 = f32[64,16]{0,1:T(8,128)S(1)} collective-permute-done((f32[64,16]{0,1:T(8,128)S(1)}, f32[64,16]{0,1:T(8,128)S(1)}, u32[]{:S(2)}, u32[]{:S(2)}) %collective-permute-start.2) | collective-permute-done | bytes 4128 | tf_op jit(solution)/shard_map/while/body/eval_jaxpr/ppermute | solution.py:18
  278.3 13.3 %collective-permute-done.2 = f32[64,16]{0,1:T(8,128)S(1)} collective-permute-done((f32[64,16]{0,1:T(8,128)S(1)}, f32[64,16]{0,1:T(8,128)S(1)}, u32[]{:S(2)}, u32[]{:S(2)}) %collective-permute-start.2) | collective-permute-done | bytes 4128 | tf_op jit(solution)/shard_map/while/body/eval_jaxpr/ppermute | solution.py:18
  297.3 13.3 %collective-permute-done.2 = f32[64,16]{0,1:T(8,128)S(1)} collective-permute-done((f32[64,16]{0,1:T(8,128)S(1)}, f32[64,16]{0,1:T(8,128)S(1)}, u32[]{:S(2)}, u32[]{:S(2)}) %collective-permute-start.2) | collective-permute-done | bytes 4128 | tf_op jit(solution)/shard_map/while/body/eval_jaxpr/ppermute | solution.py:18
  311.9 37.3 %all-gather.2.cloned.1.call-done = bf16[1024,2048]{1,0:T(8,128)(2,1)} async-done(((bf16[64,2048]{1,0:T(8,128)(2,1)}), bf16[1024,2048]{1,0:T(8,128)(2,1)}) %all-gather.2.cloned.1.call-update) | async-done | bytes 4194320 | tf_op jit(solution)/shard_map/all_gather | solution.py:110
  349.2 9.9 %fusion.31 = f32[1024,1024]{1,0:T(8,128)} fusion(bf16[1024,2048]{1,0:T(8,128)(2,1)} %all-gather.2.cloned.1.call-done, bf16[2048,1024]{1,0:T(8,128)(2,1)} %param.9), kind=kOutput, calls=%fused_computation.52 | convolution fusion | flops 4294967296 | bytes 12582912 | tf_op jit(solution)/shard_map/dot_general | solution.py:109
  359.1 84.9 %reduce-scatter.2.cloned.1.call-done = f32[128,1024]{1,0:T(8,128)} async-done(((f32[1024,1024]{1,0:T(8,128)}), f32[128,1024]{1,0:T(8,128)}) %reduce-scatter.2.cloned.1.call-update) | async-done | bytes 524304 | tf_op jit(solution)/shard_map/reduce_scatter | solution.py:114
  (328 shorter events, 88.9 us)
Async XLA Ops:
  6.5 342.6 %all-gather.2.cloned.1.call-start = ((), (), s32[]{:S(2)}) async-start(), calls=%async_computation.1 | async-start | bytes 4456448 | tf_op jit(solution)/shard_map/all_gather | solution.py:110
  12.7 13.8 %collective-permute-start.1 = (f32[64,16,128]{2,1,0:T(8,128)S(1)}, f32[64,16,128]{2,1,0:T(8,128)S(1)}, u32[]{:S(2)}, u32[]{:S(2)}) collective-permute-start(f32[64,16,128]{2,1,0:T(8,128)S(1)} %fusion.50), channel_id=1, source_target_pairs={{0,8},{8,16},{16,24},{24,32},{32,40},{40,48},{48,56},{56,64},{64,7... | collective-permute-start | bytes 1572872 | tf_op jit(solution)/shard_map/while/body/eval_jaxpr/ppermute | solution.py:18
  12.8 13.7 %collective-permute-start = (bf16[64,2048]{1,0:T(8,128)(2,1)S(1)}, bf16[64,2048]{1,0:T(8,128)(2,1)S(1)}, u32[]{:S(2)}, u32[]{:S(2)}) collective-permute-start(bf16[64,2048]{1,0:T(8,128)(2,1)S(1)} %copy.39), channel_id=1, source_target_pairs={{0,8},{8,16},{16,24},{24,32},{32,40},{40,48},{48,56},{56,64},{64,7... | collective-permute-start | bytes 786440 | tf_op jit(solution)/shard_map/while/body/eval_jaxpr/ppermute | solution.py:18
  31.7 13.8 %collective-permute-start.1 = (f32[64,16,128]{2,1,0:T(8,128)S(1)}, f32[64,16,128]{2,1,0:T(8,128)S(1)}, u32[]{:S(2)}, u32[]{:S(2)}) collective-permute-start(f32[64,16,128]{2,1,0:T(8,128)S(1)} %fusion.50), channel_id=1, source_target_pairs={{0,8},{8,16},{16,24},{24,32},{32,40},{40,48},{48,56},{56,64},{64,7... | collective-permute-start | bytes 1572872 | tf_op jit(solution)/shard_map/while/body/eval_jaxpr/ppermute | solution.py:18
  31.8 13.7 %collective-permute-start = (bf16[64,2048]{1,0:T(8,128)(2,1)S(1)}, bf16[64,2048]{1,0:T(8,128)(2,1)S(1)}, u32[]{:S(2)}, u32[]{:S(2)}) collective-permute-start(bf16[64,2048]{1,0:T(8,128)(2,1)S(1)} %copy.39), channel_id=1, source_target_pairs={{0,8},{8,16},{16,24},{24,32},{32,40},{40,48},{48,56},{56,64},{64,7... | collective-permute-start | bytes 786440 | tf_op jit(solution)/shard_map/while/body/eval_jaxpr/ppermute | solution.py:18
  50.6 13.8 %collective-permute-start.1 = (f32[64,16,128]{2,1,0:T(8,128)S(1)}, f32[64,16,128]{2,1,0:T(8,128)S(1)}, u32[]{:S(2)}, u32[]{:S(2)}) collective-permute-start(f32[64,16,128]{2,1,0:T(8,128)S(1)} %fusion.50), channel_id=1, source_target_pairs={{0,8},{8,16},{16,24},{24,32},{32,40},{40,48},{48,56},{56,64},{64,7... | collective-permute-start | bytes 1572872 | tf_op jit(solution)/shard_map/while/body/eval_jaxpr/ppermute | solution.py:18
  50.7 13.7 %collective-permute-start = (bf16[64,2048]{1,0:T(8,128)(2,1)S(1)}, bf16[64,2048]{1,0:T(8,128)(2,1)S(1)}, u32[]{:S(2)}, u32[]{:S(2)}) collective-permute-start(bf16[64,2048]{1,0:T(8,128)(2,1)S(1)} %copy.39), channel_id=1, source_target_pairs={{0,8},{8,16},{16,24},{24,32},{32,40},{40,48},{48,56},{56,64},{64,7... | collective-permute-start | bytes 786440 | tf_op jit(solution)/shard_map/while/body/eval_jaxpr/ppermute | solution.py:18
  69.6 13.8 %collective-permute-start.1 = (f32[64,16,128]{2,1,0:T(8,128)S(1)}, f32[64,16,128]{2,1,0:T(8,128)S(1)}, u32[]{:S(2)}, u32[]{:S(2)}) collective-permute-start(f32[64,16,128]{2,1,0:T(8,128)S(1)} %fusion.50), channel_id=1, source_target_pairs={{0,8},{8,16},{16,24},{24,32},{32,40},{40,48},{48,56},{56,64},{64,7... | collective-permute-start | bytes 1572872 | tf_op jit(solution)/shard_map/while/body/eval_jaxpr/ppermute | solution.py:18
  88.5 13.8 %collective-permute-start.1 = (f32[64,16,128]{2,1,0:T(8,128)S(1)}, f32[64,16,128]{2,1,0:T(8,128)S(1)}, u32[]{:S(2)}, u32[]{:S(2)}) collective-permute-start(f32[64,16,128]{2,1,0:T(8,128)S(1)} %fusion.50), channel_id=1, source_target_pairs={{0,8},{8,16},{16,24},{24,32},{32,40},{40,48},{48,56},{56,64},{64,7... | collective-permute-start | bytes 1572872 | tf_op jit(solution)/shard_map/while/body/eval_jaxpr/ppermute | solution.py:18
  88.6 13.7 %collective-permute-start = (bf16[64,2048]{1,0:T(8,128)(2,1)S(1)}, bf16[64,2048]{1,0:T(8,128)(2,1)S(1)}, u32[]{:S(2)}, u32[]{:S(2)}) collective-permute-start(bf16[64,2048]{1,0:T(8,128)(2,1)S(1)} %copy.39), channel_id=1, source_target_pairs={{0,8},{8,16},{16,24},{24,32},{32,40},{40,48},{48,56},{56,64},{64,7... | collective-permute-start | bytes 786440 | tf_op jit(solution)/shard_map/while/body/eval_jaxpr/ppermute | solution.py:18
  107.5 13.8 %collective-permute-start.1 = (f32[64,16,128]{2,1,0:T(8,128)S(1)}, f32[64,16,128]{2,1,0:T(8,128)S(1)}, u32[]{:S(2)}, u32[]{:S(2)}) collective-permute-start(f32[64,16,128]{2,1,0:T(8,128)S(1)} %fusion.50), channel_id=1, source_target_pairs={{0,8},{8,16},{16,24},{24,32},{32,40},{40,48},{48,56},{56,64},{64,7... | collective-permute-start | bytes 1572872 | tf_op jit(solution)/shard_map/while/body/eval_jaxpr/ppermute | solution.py:18
  126.4 13.8 %collective-permute-start.1 = (f32[64,16,128]{2,1,0:T(8,128)S(1)}, f32[64,16,128]{2,1,0:T(8,128)S(1)}, u32[]{:S(2)}, u32[]{:S(2)}) collective-permute-start(f32[64,16,128]{2,1,0:T(8,128)S(1)} %fusion.50), channel_id=1, source_target_pairs={{0,8},{8,16},{16,24},{24,32},{32,40},{40,48},{48,56},{56,64},{64,7... | collective-permute-start | bytes 1572872 | tf_op jit(solution)/shard_map/while/body/eval_jaxpr/ppermute | solution.py:18
  126.5 13.7 %collective-permute-start = (bf16[64,2048]{1,0:T(8,128)(2,1)S(1)}, bf16[64,2048]{1,0:T(8,128)(2,1)S(1)}, u32[]{:S(2)}, u32[]{:S(2)}) collective-permute-start(bf16[64,2048]{1,0:T(8,128)(2,1)S(1)} %copy.39), channel_id=1, source_target_pairs={{0,8},{8,16},{16,24},{24,32},{32,40},{40,48},{48,56},{56,64},{64,7... | collective-permute-start | bytes 786440 | tf_op jit(solution)/shard_map/while/body/eval_jaxpr/ppermute | solution.py:18
  145.4 13.8 %collective-permute-start.1 = (f32[64,16,128]{2,1,0:T(8,128)S(1)}, f32[64,16,128]{2,1,0:T(8,128)S(1)}, u32[]{:S(2)}, u32[]{:S(2)}) collective-permute-start(f32[64,16,128]{2,1,0:T(8,128)S(1)} %fusion.50), channel_id=1, source_target_pairs={{0,8},{8,16},{16,24},{24,32},{32,40},{40,48},{48,56},{56,64},{64,7... | collective-permute-start | bytes 1572872 | tf_op jit(solution)/shard_map/while/body/eval_jaxpr/ppermute | solution.py:18
  145.5 13.7 %collective-permute-start = (bf16[64,2048]{1,0:T(8,128)(2,1)S(1)}, bf16[64,2048]{1,0:T(8,128)(2,1)S(1)}, u32[]{:S(2)}, u32[]{:S(2)}) collective-permute-start(bf16[64,2048]{1,0:T(8,128)(2,1)S(1)} %copy.39), channel_id=1, source_target_pairs={{0,8},{8,16},{16,24},{24,32},{32,40},{40,48},{48,56},{56,64},{64,7... | collective-permute-start | bytes 786440 | tf_op jit(solution)/shard_map/while/body/eval_jaxpr/ppermute | solution.py:18
  164.3 13.8 %collective-permute-start.1 = (f32[64,16,128]{2,1,0:T(8,128)S(1)}, f32[64,16,128]{2,1,0:T(8,128)S(1)}, u32[]{:S(2)}, u32[]{:S(2)}) collective-permute-start(f32[64,16,128]{2,1,0:T(8,128)S(1)} %fusion.50), channel_id=1, source_target_pairs={{0,8},{8,16},{16,24},{24,32},{32,40},{40,48},{48,56},{56,64},{64,7... | collective-permute-start | bytes 1572872 | tf_op jit(solution)/shard_map/while/body/eval_jaxpr/ppermute | solution.py:18
  183.3 13.8 %collective-permute-start.1 = (f32[64,16,128]{2,1,0:T(8,128)S(1)}, f32[64,16,128]{2,1,0:T(8,128)S(1)}, u32[]{:S(2)}, u32[]{:S(2)}) collective-permute-start(f32[64,16,128]{2,1,0:T(8,128)S(1)} %fusion.50), channel_id=1, source_target_pairs={{0,8},{8,16},{16,24},{24,32},{32,40},{40,48},{48,56},{56,64},{64,7... | collective-permute-start | bytes 1572872 | tf_op jit(solution)/shard_map/while/body/eval_jaxpr/ppermute | solution.py:18
  202.2 13.8 %collective-permute-start.1 = (f32[64,16,128]{2,1,0:T(8,128)S(1)}, f32[64,16,128]{2,1,0:T(8,128)S(1)}, u32[]{:S(2)}, u32[]{:S(2)}) collective-permute-start(f32[64,16,128]{2,1,0:T(8,128)S(1)} %fusion.50), channel_id=1, source_target_pairs={{0,8},{8,16},{16,24},{24,32},{32,40},{40,48},{48,56},{56,64},{64,7... | collective-permute-start | bytes 1572872 | tf_op jit(solution)/shard_map/while/body/eval_jaxpr/ppermute | solution.py:18
  221.2 13.8 %collective-permute-start.1 = (f32[64,16,128]{2,1,0:T(8,128)S(1)}, f32[64,16,128]{2,1,0:T(8,128)S(1)}, u32[]{:S(2)}, u32[]{:S(2)}) collective-permute-start(f32[64,16,128]{2,1,0:T(8,128)S(1)} %fusion.50), channel_id=1, source_target_pairs={{0,8},{8,16},{16,24},{24,32},{32,40},{40,48},{48,56},{56,64},{64,7... | collective-permute-start | bytes 1572872 | tf_op jit(solution)/shard_map/while/body/eval_jaxpr/ppermute | solution.py:18
  240.1 13.8 %collective-permute-start.1 = (f32[64,16,128]{2,1,0:T(8,128)S(1)}, f32[64,16,128]{2,1,0:T(8,128)S(1)}, u32[]{:S(2)}, u32[]{:S(2)}) collective-permute-start(f32[64,16,128]{2,1,0:T(8,128)S(1)} %fusion.50), channel_id=1, source_target_pairs={{0,8},{8,16},{16,24},{24,32},{32,40},{40,48},{48,56},{56,64},{64,7... | collective-permute-start | bytes 1572872 | tf_op jit(solution)/shard_map/while/body/eval_jaxpr/ppermute | solution.py:18
  259.1 13.8 %collective-permute-start.1 = (f32[64,16,128]{2,1,0:T(8,128)S(1)}, f32[64,16,128]{2,1,0:T(8,128)S(1)}, u32[]{:S(2)}, u32[]{:S(2)}) collective-permute-start(f32[64,16,128]{2,1,0:T(8,128)S(1)} %fusion.50), channel_id=1, source_target_pairs={{0,8},{8,16},{16,24},{24,32},{32,40},{40,48},{48,56},{56,64},{64,7... | collective-permute-start | bytes 1572872 | tf_op jit(solution)/shard_map/while/body/eval_jaxpr/ppermute | solution.py:18
  278.0 13.8 %collective-permute-start.1 = (f32[64,16,128]{2,1,0:T(8,128)S(1)}, f32[64,16,128]{2,1,0:T(8,128)S(1)}, u32[]{:S(2)}, u32[]{:S(2)}) collective-permute-start(f32[64,16,128]{2,1,0:T(8,128)S(1)} %fusion.50), channel_id=1, source_target_pairs={{0,8},{8,16},{16,24},{24,32},{32,40},{40,48},{48,56},{56,64},{64,7... | collective-permute-start | bytes 1572872 | tf_op jit(solution)/shard_map/while/body/eval_jaxpr/ppermute | solution.py:18
  296.9 13.8 %collective-permute-start.1 = (f32[64,16,128]{2,1,0:T(8,128)S(1)}, f32[64,16,128]{2,1,0:T(8,128)S(1)}, u32[]{:S(2)}, u32[]{:S(2)}) collective-permute-start(f32[64,16,128]{2,1,0:T(8,128)S(1)} %fusion.50), channel_id=1, source_target_pairs={{0,8},{8,16},{16,24},{24,32},{32,40},{40,48},{48,56},{56,64},{64,7... | collective-permute-start | bytes 1572872 | tf_op jit(solution)/shard_map/while/body/eval_jaxpr/ppermute | solution.py:18
  311.8 132.2 %reduce-scatter.2.cloned.1.call-start = ((), (), s32[]{:S(2)}) async-start(), calls=%async_computation.2 | async-start | bytes 4718592 | tf_op jit(solution)/shard_map/reduce_scatter | solution.py:114
  (58 other events, 617.7 us)
Sparse Core Ops, SparseCore 0:
  311.9 37.1 all-gather.1
  359.2 84.7 reduce-scatter.1
where the time goes:
time: 453 us
  waiting for transfers between devices  333 us (74%)
  matrix products  58.4 us (13%)
  other arithmetic  32.3 us (7%)
  between operations  13.4 us (3%)
  starting transfers between devices  9.16 us (2%)
  local copies, waits for them, and re-layouts  4.89 us (1%)
    ppermute x64, waiting for transfers between devices, passed_along(): return lax.ppermute(value, axis, pairs)  211 us
    reduce_scatter x1, waiting for transfers between devices, body(): lax.psum_scatter(terms, 'head', scatter_dimension=0, tiled=True)  84.9 us
    all_gather x1, waiting for transfers between devices, body(): lax.all_gather(attended, 'ctx', axis=0, tiled=True)  37.3 us
    dot_general x16, matrix products, attend(): jnp.einsum('tkgd,ckd->tkgc', grouped, key_view, preferred_element_type=jn...  29.9 us
    reduce_sum x16, other arithmetic, attend(): weight_sum = jnp.sum(weights, axis=-1)  21.4 us
    dot_general x16, matrix products, attend(): jnp.einsum('tkgc,ckd->tkgd', weights.astype(jnp.bfloat16), value_view, pr...  18.6 us
    dot_general x1, matrix products, body(): jnp.dot(lax.all_gather(attended, 'ctx', axis=0, tiled=True), out_weight,...  9.88 us
    ppermute x64, starting transfers between devices, passed_along(): return lax.ppermute(value, axis, pairs)  9.12 us
  transfers between devices with their start and end apart: 66, of which 34 were waited for; matrix products, arithmetic and copies ran while one was open for 0% of the time, Pallas kernels for 0%

commit v1 on v0

v1 whole, which is shorter than its diff:
```python
import math

import jax
import jax.numpy as jnp
from jax import lax
from jax.experimental import pallas as pl
from jax.experimental.pallas import tpu as pltpu
from jax.sharding import PartitionSpec as P

HD = 128
RUN = 64
NEG = -1e30
ROWS = 256
KEYS = 512
LOG2E = math.log2(math.e)
MESH = pl.DeviceIdType.MESH

S_KV = 0
S_Q = 14
S_O = 15
S_STAT = 16
S_ATT = 17
S_FAR = 34
S_NEAR = 38
S_SIDE = 42
S_COUNT = 43


def device_at(x, y, core):
    return x * 8 + y * 2 + core


def kernel(
    q_ref, k_ref, v_ref, w_hbm, out_ref,
    q_t, kv, acc, mrow, lrow, o_send, s_send, o_recv, s_recv, att, w,
    far, far_in, near, near_in, side, side_in, total, w_sem, send, recv,
):
    c, h = lax.axis_index("ctx"), lax.axis_index("head")
    x, y, core = c // 8, (c // 2) % 4, c % 2
    z, e = h // 2, h % 2
    scale = LOG2E / math.sqrt(HD)

    to_core = (device_at(x, y, 1 - core), h)
    to_up = (device_at(x, (y + 1) % 4, core), h)
    to_down = (device_at(x, (y + 3) % 4, core), h)
    to_x = (device_at(1 - x, y, core), h)
    to_zup = (c, ((z + 1) % 4) * 2 + e)
    to_zdown = (c, ((z + 3) % 4) * 2 + e)
    to_side = (c, z * 2 + 1 - e)
    partners = (to_core, to_up, to_down, to_x, to_zup, to_zdown, to_side)

    def remote(src, dst, number, where):
        return pltpu.make_async_remote_copy(
            src_ref=src, dst_ref=dst, send_sem=send.at[number], recv_sem=recv.at[number],
            device_id=where, device_id_type=MESH,
        )

    w_copy = pltpu.make_async_copy(w_hbm, w, w_sem)
    w_copy.start()
    barrier = pltpu.get_barrier_semaphore()
    for partner in partners:
        pl.semaphore_signal(barrier, inc=1, device_id=partner, device_id_type=MESH)

    for r in range(4):
        half, group = r // 2, r % 2
        heads = [
            q_ref[half * 32 : half * 32 + 32, (group * 8 + i) * HD : (group * 8 + i + 1) * HD]
            for i in range(8)
        ]
        block = jnp.concatenate(heads, axis=0).astype(jnp.float32)
        q_t[r] = block.T.astype(jnp.bfloat16)
    for half in range(2):
        kv[half, 0:KEYS] = k_ref[half * KEYS : (half + 1) * KEYS]
        for b in range(4):
            start = half * KEYS + b * HD
            piece = v_ref[start : start + HD].astype(jnp.float32)
            kv[half, KEYS + b * HD : KEYS + (b + 1) * HD] = piece.T.astype(jnp.bfloat16)
    for r in range(8):
        acc[r] = jnp.zeros((HD, ROWS), jnp.float32)
        mrow[r] = jnp.full((1, ROWS), NEG, jnp.float32)
        lrow[r] = jnp.zeros((1, ROWS), jnp.float32)

    pl.semaphore_wait(barrier, len(partners))

    def kv_copy(number, source, target, where):
        return remote(kv.at[source], kv.at[target], S_KV + number, where)

    own_up = [kv_copy(0 + i, i, 12 + i, to_up) for i in range(2)]
    own_down = [kv_copy(2 + i, i, 4 + i, to_down) for i in range(2)]
    own_core = [kv_copy(4 + i, i, 2 + i, to_core) for i in range(2)]
    pass_12 = kv_copy(6, 12, 14, to_core)
    pass_4 = kv_copy(7, 4, 6, to_core)
    pass_13 = kv_copy(8, 13, 15, to_core)
    pass_5 = kv_copy(9, 5, 7, to_core)
    on_up = kv_copy(10, 12, 8, to_up)
    on_down = kv_copy(11, 5, 9, to_down)
    pass_8 = kv_copy(12, 8, 10, to_core)
    pass_9 = kv_copy(13, 9, 11, to_core)
    q_copy = remote(q_t.at[0:4], q_t.at[4:8], S_Q, to_x)
    o_copy = remote(o_send, o_recv, S_O, to_x)
    s_copy = remote(s_send, s_recv, S_STAT, to_x)

    q_copy.start()
    for i in range(2):
        own_up[i].start()
        own_down[i].start()
        own_core[i].start()

    def finish_neighbour():
        row = lax.broadcasted_iota(jnp.int32, (8, ROWS), 0)
        for r in range(4):
            o_send[r] = (acc[4 + r] / lrow[4 + r]).astype(jnp.bfloat16)
            s_send[r] = jnp.where(row == 0, mrow[4 + r], lrow[4 + r])
        o_copy.start()
        s_copy.start()

    def unit(u, carry):
        @pl.when(u == 2)
        def _():
            own_core[0].wait_recv()
            own_core[1].wait_recv()

        @pl.when(u == 4)
        def _():
            q_copy.wait_recv()

        @pl.when(u == 8)
        def _():
            own_up[0].wait_recv()
            on_up.start()
            pass_12.start()
            own_down[0].wait_recv()
            pass_4.start()

        @pl.when(u == 10)
        def _():
            pass_12.wait_recv()
            pass_4.wait_recv()

        @pl.when(u == 16)
        def _():
            own_down[1].wait_recv()
            on_down.start()
            pass_5.start()
            own_up[1].wait_recv()
            pass_13.start()

        @pl.when(u == 18)
        def _():
            pass_13.wait_recv()
            pass_5.wait_recv()

        @pl.when(u == 24)
        def _():
            on_up.wait_recv()
            pass_8.start()
            on_down.wait_recv()
            pass_9.start()

        @pl.when(u == 26)
        def _():
            pass_8.wait_recv()
            pass_9.wait_recv()

        @pl.when(u == 28)
        def _():
            finish_neighbour()

        stage, v = u // 8, u % 8
        i = v % 4
        group = jnp.where(stage == 3, 1 - v // 4, v // 4)
        middle = 12 - 8 * (i % 2) + 2 * (i // 2) + stage - 1
        slot = jnp.where(stage == 0, i, jnp.where(stage == 3, 8 + i, middle))
        holder_core = jnp.where((slot // 2) % 2 == 1, 1 - core, core)
        holder = device_at(x, (y + slot // 4) % 4, holder_core)
        key_base = jnp.where(slot % 2 == 1, holder * RUN, -(1 << 20))
        asker = device_at(jnp.where(group == 1, 1 - x, x), y, core)
        key_rel = key_base - asker * RUN + lax.broadcasted_iota(jnp.int32, (RUN, ROWS), 0)
        token = lax.broadcasted_iota(jnp.int32, (RUN, ROWS), 1) % 32

        keys = kv[slot, 0:KEYS]
        values = jnp.concatenate(
            [kv[slot, KEYS + b * HD : KEYS + (b + 1) * HD] for b in range(4)], axis=1
        )

        def scores_of(r):
            return jnp.dot(keys, q_t[group * 4 + r], preferred_element_type=jnp.float32) * scale

        scores = scores_of(0)
        for r in range(4):
            row = group * 4 + r
            later = scores_of(r + 1) if r < 3 else None
            tail = jnp.where(key_rel <= token + (r // 2) * 32, scores[KEYS - RUN :], NEG)
            scores = jnp.concatenate([scores[: KEYS - RUN], tail], axis=0)
            old = mrow[row]
            new = jnp.maximum(old, jnp.max(scores, axis=0, keepdims=True))
            weights = jnp.exp2(scores - new)
            fade = jnp.exp2(old - new)
            mrow[row] = new
            lrow[row] = lrow[row] * fade + jnp.sum(weights, axis=0, keepdims=True)
            acc[row] = acc[row] * fade + jnp.dot(
                values, weights.astype(jnp.bfloat16), preferred_element_type=jnp.float32
            )
            scores = later
        return carry

    lax.fori_loop(0, 32, unit, 0)

    o_copy.wait_recv()
    s_copy.wait_recv()
    for r in range(4):
        half, group = r // 2, r % 2
        m_b, l_b = s_recv[r, 0:1], s_recv[r, 1:2]
        new = jnp.maximum(mrow[r], m_b)
        fade_a = jnp.exp2(mrow[r] - new)
        fade_b = jnp.exp2(m_b - new) * l_b
        summed = acc[r] * fade_a + o_recv[r].astype(jnp.float32) * fade_b
        done = (summed / (lrow[r] * fade_a + fade_b)).T.astype(jnp.bfloat16)
        for i in range(8):
            head = group * 8 + i
            att[0, 0, half * 32 : half * 32 + 32, head * HD : (head + 1) * HD] = done[
                i * 32 : i * 32 + 32
            ]

    def att_copy(number, source, target, where):
        return remote(att.at[source, 0], att.at[target, 0], S_ATT + number, where)

    def att_core(number, slot):
        return remote(att.at[slot, 0], att.at[slot, 1], S_ATT + number, to_core)

    def att_half(number, source, target, half, where):
        rows = pl.ds(half * 32, 32)
        return remote(
            att.at[source, 0, rows], att.at[target, 0, rows], S_ATT + number, where
        )

    a_core = [att_core(slot, slot) for slot in range(8)]
    a_x = att_copy(8, 0, 4, to_x)
    a_up = [att_copy(9, 0, 3, to_up), att_copy(10, 4, 7, to_up)]
    a_down = [att_copy(11, 0, 1, to_down), att_copy(12, 4, 5, to_down)]
    a_up2 = [att_half(13, 3, 2, 0, to_up), att_half(14, 7, 6, 0, to_up)]
    a_down2 = [att_half(15, 1, 2, 1, to_down), att_half(16, 5, 6, 1, to_down)]

    a_x.start()
    a_up[0].start()
    a_down[0].start()
    a_core[0].start()
    a_x.wait_recv()
    a_up[1].start()
    a_down[1].start()
    a_core[4].start()
    for plane in range(2):
        a_up[plane].wait_recv()
        a_up2[plane].start()
        a_core[plane * 4 + 3].start()
        a_down[plane].wait_recv()
        a_down2[plane].start()
        a_core[plane * 4 + 1].start()
    for plane in range(2):
        a_up2[plane].wait_recv()
        a_down2[plane].wait_recv()
        a_core[plane * 4 + 2].start()
    w_copy.wait()
    for slot in range(8):
        a_core[slot].wait_recv()

    cols = w.shape[1] // 2

    def project(distance, side_of, part):
        target = ((z + distance) % 4) * 2 + side_of
        slot = jnp.where(target // 4 == x, 0, 4) + (target % 4 - y + 4) % 4
        block = jnp.concatenate([att[slot, core], att[slot, 1 - core]], axis=0)
        return jnp.dot(
            block, w[:, part * cols : (part + 1) * cols], preferred_element_type=jnp.float32
        )

    def far_copy(way, s):
        return remote(
            far.at[way, s], far_in.at[way, s], S_FAR + way * 2 + s, (to_zup, to_zdown)[way]
        )

    def near_copy(way, s):
        return remote(
            near.at[way, s], near_in.at[way, s], S_NEAR + way * 2 + s, (to_zup, to_zdown)[way]
        )

    side_copy = remote(side, side_in, S_SIDE, to_side)

    def far_step(s, carry):
        for way in range(2):
            far[way, s] = project(2, s, way).astype(jnp.bfloat16)
            far_copy(way, s).start()
        return carry

    lax.fori_loop(0, 2, far_step, 0)
    for way in range(2):

        def near_step(s, carry):
            other = 1 - way
            near[way, s, :, other * cols : (other + 1) * cols] = project(
                1 + 2 * way, s, other
            ).astype(jnp.bfloat16)
            far_copy(way, s).wait_recv()
            near[way, s, :, way * cols : (way + 1) * cols] = (
                project(1 + 2 * way, s, way) + far_in[way, s].astype(jnp.float32)
            ).astype(jnp.bfloat16)
            near_copy(way, s).start()
            return carry

        lax.fori_loop(0, 2, near_step, 0)

    def last_step(turn, carry):
        s = jnp.where(turn == 0, 1 - e, e)
        for part in range(2):
            total[:, part * cols : (part + 1) * cols] = project(0, s, part)
        near_copy(0, s).wait_recv()
        near_copy(1, s).wait_recv()
        total[...] = (
            total[...] + near_in[0, s].astype(jnp.float32) + near_in[1, s].astype(jnp.float32)
        )

        @pl.when(turn == 0)
        def _():
            side[...] = total[...].astype(jnp.bfloat16)
            side_copy.start()

        return carry

    lax.fori_loop(0, 2, last_step, 0)
    side_copy.wait_recv()
    out_ref[...] = (total[...] + side_in[...].astype(jnp.float32)).astype(jnp.bfloat16)

    sent = own_up + own_down + own_core + [pass_12, pass_4, pass_13, pass_5, on_up, on_down]
    sent += [pass_8, pass_9, q_copy, o_copy, s_copy, a_x, side_copy]
    sent += a_core + a_up + a_down + a_up2 + a_down2
    sent += [far_copy(way, s) for way in range(2) for s in range(2)]
    sent += [near_copy(way, s) for way in range(2) for s in range(2)]
    for copy in sent:
        copy.wait_send()


def body(queries, key_cache, value_cache, out_weight):
    tokens, width = queries.shape
    cols = out_weight.shape[1]
    vmem = pl.BlockSpec(memory_space=pltpu.VMEM)
    bf16, f32 = jnp.bfloat16, jnp.float32
    return pl.pallas_call(
        kernel,
        out_shape=jax.ShapeDtypeStruct((2 * tokens, cols), bf16),
        in_specs=[vmem, vmem, vmem, pl.BlockSpec(memory_space=pl.ANY)],
        out_specs=vmem,
        scratch_shapes=[
            pltpu.VMEM((8, HD, ROWS), bf16),
            pltpu.VMEM((16, 2 * KEYS, HD), bf16),
            pltpu.VMEM((8, HD, ROWS), f32),
            pltpu.VMEM((8, 1, ROWS), f32),
            pltpu.VMEM((8, 1, ROWS), f32),
            pltpu.VMEM((4, HD, ROWS), bf16),
            pltpu.VMEM((4, 8, ROWS), f32),
            pltpu.VMEM((4, HD, ROWS), bf16),
            pltpu.VMEM((4, 8, ROWS), f32),
            pltpu.VMEM((8, 2, tokens, width), bf16),
            pltpu.VMEM(out_weight.shape, bf16),
            pltpu.VMEM((2, 2, 2 * tokens, cols // 2), bf16),
            pltpu.VMEM((2, 2, 2 * tokens, cols // 2), bf16),
            pltpu.VMEM((2, 2, 2 * tokens, cols), bf16),
            pltpu.VMEM((2, 2, 2 * tokens, cols), bf16),
            pltpu.VMEM((2 * tokens, cols), bf16),
            pltpu.VMEM((2 * tokens, cols), bf16),
            pltpu.VMEM((2 * tokens, cols), f32),
            pltpu.SemaphoreType.DMA,
            pltpu.SemaphoreType.DMA((S_COUNT,)),
            pltpu.SemaphoreType.DMA((S_COUNT,)),
        ],
        compiler_params=pltpu.CompilerParams(
            collective_id=0, has_side_effects=True, vmem_limit_bytes=56 * 1024 * 1024
        ),
        cost_estimate=pl.CostEstimate(
            flops=13_000_000_000, bytes_accessed=5_000_000, transcendentals=17_000_000
        ),
    )(queries, key_cache, value_cache, out_weight)


def solution(mesh):
    in_specs = (P("ctx", "head"), P("ctx", "head"), P("ctx", "head"), P("head", "ctx"))
    out_specs = P("head", "ctx")
    return jax.shard_map(body, mesh=mesh, in_specs=in_specs, out_specs=out_specs, check_vma=False)
```

time: 453 us -> 104 us (0.23)
  waiting for transfers between devices: 333 us -> 0 us
  Pallas kernels: 0 us -> 101 us
  matrix products: 58.4 us -> 0 us
  other arithmetic: 32.3 us -> 0 us
  between operations: 13.4 us -> 0.01 us
  starting transfers between devices: 9.16 us -> 0 us
    ppermute x64 -> x0, waiting for transfers between devices: 211 us -> none  [passed_along(): return lax.ppermute(value, axis, pairs)]
    pallas_call x0 -> x1, Pallas kernels: none -> 101 us  [body(): pl.pallas_call(kernel, out_shape=jax.ShapeDtypeStruct((2 * tokens, cols),...]
    reduce_scatter x1 -> x0, waiting for transfers between devices: 84.9 us -> none  [body(): lax.psum_scatter(terms, 'head', scatter_dimension=0, tiled=True)]
    dot_general x33 -> x0, matrix products: 58.4 us -> none  [the longest x16 29.9 us: attend(): jnp.einsum('tkgd,ckd->tkgc', grouped, key_view, preferred_element_type=jn...]
    all_gather x1 -> x0, waiting for transfers between devices: 37.3 us -> none  [body(): lax.all_gather(attended, 'ctx', axis=0, tiled=True)]
    reduce_sum x16 -> x0, other arithmetic: 21.4 us -> none  [attend(): weight_sum = jnp.sum(weights, axis=-1)]
    ppermute x64 -> x0, starting transfers between devices: 9.12 us -> none  [passed_along(): return lax.ppermute(value, axis, pairs)]
    add x64 -> x0, other arithmetic: 7.22 us -> none  [the longest x16 6.56 us: combine(): summed_a * scale_a[..., None] + summed_b * scale_b[..., None]]
  transfers between devices with their start and end apart: 66 -> 0, of which waited for: 34 -> 0; matrix products, arithmetic and copies ran while one was open for 0% -> 0% of each run, Pallas kernels for 0% -> 0%
where the time goes in v1:
time: 104 us; the launch traced here: 103 us
  Pallas kernels  101 us (97%)
  local copies, waits for them, and re-layouts  1.67 us (2%)
    pallas_call x1, Pallas kernels, body(): pl.pallas_call(kernel, out_shape=jax.ShapeDtypeStruct((2 * tokens, cols),...  101 us

profile of v1, /device:TPU:0, one launch (start us, length us, event | category | flops | bytes accessed | tf_op | source)
XLA Modules:
  0.0 102.5 jit_solution(16533926241442651306)
XLA Ops:
  0.0 100.8 %shard_map.46 = bf16[128,1024]{1,0:T(8,128)(2,1)} custom-call(bf16[64,2048]{1,0:T(8,128)(2,1)} %q_ref.1, bf16[1024,128]{1,0:T(8,128)(2,1)} %k_ref.1, bf16[1024,128]{1,0:T(8,128)(2,1)} %v_ref.1, bf16[2048,1024]{1,0:T(8,128)(2,1)} %w_hbm.1), custom_call_target="tpu_custom_call" | custom-call | flops 12999999488 | bytes 5000000 | tf_op jit(solution)/shard_map/pallas_call | solution.py:347
  100.8 1.7 %copy.6 = bf16[128,1024]{1,0:T(8,128)(2,1)} copy(bf16[128,1024]{1,0:T(8,128)(2,1)} %shard_map.46) | data formatting | bytes 524288

commit v2 on v1

--- a/solution.py
+++ b/solution.py
@@ -10,7 +10,7 @@
 HD = 128
 RUN = 64
 NEG = -1e30
-ROWS = 256
+ROWS = 512
 KEYS = 512
 LOG2E = math.log2(math.e)
 MESH = pl.DeviceIdType.MESH
@@ -32,7 +32,7 @@
 
 def kernel(
     q_ref, k_ref, v_ref, w_hbm, out_ref,
-    q_t, kv, acc, mrow, lrow, o_send, s_send, o_recv, s_recv, att, w,
+    q_t, kv, s0, s1, p1, fade1, acc, mrow, lrow, o_send, s_send, o_recv, s_recv, att, w,
     far, far_in, near, near_in, side, side_in, total, w_sem, send, recv,
 ):
     c, h = lax.axis_index("ctx"), lax.axis_index("head")
@@ -61,12 +61,8 @@
     for partner in partners:
         pl.semaphore_signal(barrier, inc=1, device_id=partner, device_id_type=MESH)
 
-    for r in range(4):
-        half, group = r // 2, r % 2
-        heads = [
-            q_ref[half * 32 : half * 32 + 32, (group * 8 + i) * HD : (group * 8 + i + 1) * HD]
-            for i in range(8)
-        ]
+    for r in range(2):
+        heads = [q_ref[r * 32 : r * 32 + 32, i * HD : (i + 1) * HD] for i in range(16)]
         block = jnp.concatenate(heads, axis=0).astype(jnp.float32)
         q_t[r] = block.T.astype(jnp.bfloat16)
     for half in range(2):
@@ -75,7 +71,7 @@
             start = half * KEYS + b * HD
             piece = v_ref[start : start + HD].astype(jnp.float32)
             kv[half, KEYS + b * HD : KEYS + (b + 1) * HD] = piece.T.astype(jnp.bfloat16)
-    for r in range(8):
+    for r in range(4):
         acc[r] = jnp.zeros((HD, ROWS), jnp.float32)
         mrow[r] = jnp.full((1, ROWS), NEG, jnp.float32)
         lrow[r] = jnp.zeros((1, ROWS), jnp.float32)
@@ -96,7 +92,7 @@
     on_down = kv_copy(11, 5, 9, to_down)
     pass_8 = kv_copy(12, 8, 10, to_core)
     pass_9 = kv_copy(13, 9, 11, to_core)
-    q_copy = remote(q_t.at[0:4], q_t.at[4:8], S_Q, to_x)
+    q_copy = remote(q_t.at[0:2], q_t.at[2:4], S_Q, to_x)
     o_copy = remote(o_send, o_recv, S_O, to_x)
     s_copy = remote(s_send, s_recv, S_STAT, to_x)
 
@@ -108,119 +104,134 @@
 
     def finish_neighbour():
         row = lax.broadcasted_iota(jnp.int32, (8, ROWS), 0)
-        for r in range(4):
-            o_send[r] = (acc[4 + r] / lrow[4 + r]).astype(jnp.bfloat16)
-            s_send[r] = jnp.where(row == 0, mrow[4 + r], lrow[4 + r])
+        for r in range(2):
+            o_send[r] = (acc[2 + r] / lrow[2 + r]).astype(jnp.bfloat16)
+            s_send[r] = jnp.where(row == 0, mrow[2 + r], lrow[2 + r])
         o_copy.start()
         s_copy.start()
 
-    def unit(u, carry):
-        @pl.when(u == 2)
-        def _():
-            own_core[0].wait_recv()
-            own_core[1].wait_recv()
-
-        @pl.when(u == 4)
-        def _():
-            q_copy.wait_recv()
-
-        @pl.when(u == 8)
-        def _():
-            own_up[0].wait_recv()
-            on_up.start()
-            pass_12.start()
-            own_down[0].wait_recv()
-            pass_4.start()
-
-        @pl.when(u == 10)
-        def _():
-            pass_12.wait_recv()
-            pass_4.wait_recv()
-
-        @pl.when(u == 16)
-        def _():
-            own_down[1].wait_recv()
-            on_down.start()
-            pass_5.start()
-            own_up[1].wait_recv()
-            pass_13.start()
-
-        @pl.when(u == 18)
-        def _():
-            pass_13.wait_recv()
-            pass_5.wait_recv()
-
-        @pl.when(u == 24)
-        def _():
-            on_up.wait_recv()
-            pass_8.start()
-            on_down.wait_recv()
-            pass_9.start()
-
-        @pl.when(u == 26)
-        def _():
-            pass_8.wait_recv()
-            pass_9.wait_recv()
-
-        @pl.when(u == 28)
-        def _():
-            finish_neighbour()
-
+    def place(u):
         stage, v = u // 8, u % 8
         i = v % 4
         group = jnp.where(stage == 3, 1 - v // 4, v // 4)
         middle = 12 - 8 * (i % 2) + 2 * (i // 2) + stage - 1
         slot = jnp.where(stage == 0, i, jnp.where(stage == 3, 8 + i, middle))
+        return slot, group
+
+    def score(u, r, s_ref):
+        slot, group = place(u)
+        s_ref[...] = (
+            jnp.dot(kv[slot, 0:KEYS], q_t[group * 2 + r], preferred_element_type=jnp.float32)
+            * scale
+        )
+
+    def weigh(u, r, s_ref):
+        slot, group = place(u)
+        row = group * 2 + r
         holder_core = jnp.where((slot // 2) % 2 == 1, 1 - core, core)
         holder = device_at(x, (y + slot // 4) % 4, holder_core)
         key_base = jnp.where(slot % 2 == 1, holder * RUN, -(1 << 20))
         asker = device_at(jnp.where(group == 1, 1 - x, x), y, core)
         key_rel = key_base - asker * RUN + lax.broadcasted_iota(jnp.int32, (RUN, ROWS), 0)
         token = lax.broadcasted_iota(jnp.int32, (RUN, ROWS), 1) % 32
-
-        keys = kv[slot, 0:KEYS]
+        tail = jnp.where(key_rel <= token + r * 32, s_ref[KEYS - RUN :], NEG)
+        scores = jnp.concatenate([s_ref[0 : KEYS - RUN], tail], axis=0)
+        old = mrow[row]
+        new = jnp.maximum(old, jnp.max(scores, axis=0, keepdims=True))
+        weights = jnp.exp2(scores - new)
+        fade = jnp.exp2(old - new)
+        mrow[row] = new
+        lrow[row] = lrow[row] * fade + jnp.sum(weights, axis=0, keepdims=True)
+        return weights.astype(jnp.bfloat16), fade
+
+    def add_values(u, r, weights, fade):
+        slot, group = place(u)
+        row = group * 2 + r
         values = jnp.concatenate(
             [kv[slot, KEYS + b * HD : KEYS + (b + 1) * HD] for b in range(4)], axis=1
         )
-
-        def scores_of(r):
-            return jnp.dot(keys, q_t[group * 4 + r], preferred_element_type=jnp.float32) * scale
-
-        scores = scores_of(0)
-        for r in range(4):
-            row = group * 4 + r
-            later = scores_of(r + 1) if r < 3 else None
-            tail = jnp.where(key_rel <= token + (r // 2) * 32, scores[KEYS - RUN :], NEG)
-            scores = jnp.concatenate([scores[: KEYS - RUN], tail], axis=0)
-            old = mrow[row]
-            new = jnp.maximum(old, jnp.max(scores, axis=0, keepdims=True))
-            weights = jnp.exp2(scores - new)
-            fade = jnp.exp2(old - new)
-            mrow[row] = new
-            lrow[row] = lrow[row] * fade + jnp.sum(weights, axis=0, keepdims=True)
-            acc[row] = acc[row] * fade + jnp.dot(
-                values, weights.astype(jnp.bfloat16), preferred_element_type=jnp.float32
-            )
-            scores = later
+        acc[row] = acc[row] * fade + jnp.dot(values, weights, preferred_element_type=jnp.float32)
+
+    def unit(u, carry):
+        @pl.when(u == 1)
+        def _():
+            own_core[0].wait_recv()
+            own_core[1].wait_recv()
+
+        @pl.when(u == 3)
+        def _():
+            q_copy.wait_recv()
+
+        @pl.when(u == 7)
+        def _():
+            own_up[0].wait_recv()
+            on_up.start()
+            pass_12.start()
+            own_down[0].wait_recv()
+            pass_4.start()
+
+        @pl.when(u == 9)
+        def _():
+            pass_12.wait_recv()
+            pass_4.wait_recv()
+
+        @pl.when(u == 15)
+        def _():
+            own_down[1].wait_recv()
+            on_down.start()
+            pass_5.start()
+            own_up[1].wait_recv()
+            pass_13.start()
+
+        @pl.when(u == 17)
+        def _():
+            pass_13.wait_recv()
+            pass_5.wait_recv()
+
+        @pl.when(u == 23)
+        def _():
+            on_up.wait_recv()
+            pass_8.start()
+            on_down.wait_recv()
+            pass_9.start()
+
+        @pl.when(u == 25)
+        def _():
+            pass_8.wait_recv()
+            pass_9.wait_recv()
+
+        score(u, 1, s1)
+        weights, fade = weigh(u, 0, s0)
+        add_values(jnp.maximum(u - 1, 0), 1, p1[...], fade1[...])
+        score(jnp.minimum(u + 1, 31), 0, s0)
+        weights_1, fade_1 = weigh(u, 1, s1)
+        add_values(u, 0, weights, fade)
+        p1[...] = weights_1
+        fade1[...] = fade_1
+
+        @pl.when(u == 28)
+        def _():
+            finish_neighbour()
+
         return carry
 
+    p1[...] = jnp.zeros_like(p1)
+    fade1[...] = jnp.ones_like(fade1)
+    score(0, 0, s0)
     lax.fori_loop(0, 32, unit, 0)
+    add_values(31, 1, p1[...], fade1[...])
 
     o_copy.wait_recv()
     s_copy.wait_recv()
-    for r in range(4):
-        half, group = r // 2, r % 2
+    for r in range(2):
         m_b, l_b = s_recv[r, 0:1], s_recv[r, 1:2]
         new = jnp.maximum(mrow[r], m_b)
         fade_a = jnp.exp2(mrow[r] - new)
         fade_b = jnp.exp2(m_b - new) * l_b
         summed = acc[r] * fade_a + o_recv[r].astype(jnp.float32) * fade_b
         done = (summed / (lrow[r] * fade_a + fade_b)).T.astype(jnp.bfloat16)
-        for i in range(8):
-            head = group * 8 + i
-            att[0, 0, half * 32 : half * 32 + 32, head * HD : (head + 1) * HD] = done[
-                i * 32 : i * 32 + 32
-            ]
+        for i in range(16):
+            att[0, 0, r * 32 : r * 32 + 32, i * HD : (i + 1) * HD] = done[i * 32 : i * 32 + 32]
 
     def att_copy(number, source, target, where):
         return remote(att.at[source, 0], att.at[target, 0], S_ATT + number, where)
@@ -350,15 +361,19 @@
         in_specs=[vmem, vmem, vmem, pl.BlockSpec(memory_space=pl.ANY)],
         out_specs=vmem,
         scratch_shapes=[
-            pltpu.VMEM((8, HD, ROWS), bf16),
+            pltpu.VMEM((4, HD, ROWS), bf16),
             pltpu.VMEM((16, 2 * KEYS, HD), bf16),
-            pltpu.VMEM((8, HD, ROWS), f32),
-            pltpu.VMEM((8, 1, ROWS), f32),
-            pltpu.VMEM((8, 1, ROWS), f32),
-            pltpu.VMEM((4, HD, ROWS), bf16),
-            pltpu.VMEM((4, 8, ROWS), f32),
-            pltpu.VMEM((4, HD, ROWS), bf16),
-            pltpu.VMEM((4, 8, ROWS), f32),
+            pltpu.VMEM((KEYS, ROWS), f32),
+            pltpu.VMEM((KEYS, ROWS), f32),
+            pltpu.VMEM((KEYS, ROWS), bf16),
+            pltpu.VMEM((1, ROWS), f32),
+            pltpu.VMEM((4, HD, ROWS), f32),
+            pltpu.VMEM((4, 1, ROWS), f32),
+            pltpu.VMEM((4, 1, ROWS), f32),
+            pltpu.VMEM((2, HD, ROWS), bf16),
+            pltpu.VMEM((2, 8, ROWS), f32),
+            pltpu.VMEM((2, HD, ROWS), bf16),
+            pltpu.VMEM((2, 8, ROWS), f32),
             pltpu.VMEM((8, 2, tokens, width), bf16),
             pltpu.VMEM(out_weight.shape, bf16),
             pltpu.VMEM((2, 2, 2 * tokens, cols // 2), bf16),

time: 104 us -> 102 us (0.981)
  Pallas kernels: 101 us -> 98.9 us
    pallas_call x1, Pallas kernels: 101 us -> 98.9 us  [body(): pl.pallas_call(kernel, out_shape=jax.ShapeDtypeStruct((2 * tokens, cols),...]
where the time goes in v2:
time: 102 us; the launch traced here: 101 us
  Pallas kernels  98.9 us (97%)
  local copies, waits for them, and re-layouts  1.67 us (2%)
    pallas_call x1, Pallas kernels, body(): pl.pallas_call(kernel, out_shape=jax.ShapeDtypeStruct((2 * tokens, cols),...  98.9 us

profile of v2, /device:TPU:0, one launch (start us, length us, event | category | flops | bytes accessed | tf_op | source)
XLA Modules:
  0.0 100.5 jit_solution(9038190657886459971)
XLA Ops:
  0.0 98.9 %shard_map.46 = bf16[128,1024]{1,0:T(8,128)(2,1)} custom-call(bf16[64,2048]{1,0:T(8,128)(2,1)} %q_ref.1, bf16[1024,128]{1,0:T(8,128)(2,1)} %k_ref.1, bf16[1024,128]{1,0:T(8,128)(2,1)} %v_ref.1, bf16[2048,1024]{1,0:T(8,128)(2,1)} %w_hbm.1), custom_call_target="tpu_custom_call" | custom-call | flops 12999999488 | bytes 5000000 | tf_op jit(solution)/shard_map/pallas_call | solution.py:358
  98.9 1.7 %copy.6 = bf16[128,1024]{1,0:T(8,128)(2,1)} copy(bf16[128,1024]{1,0:T(8,128)(2,1)} %shard_map.46) | data formatting | bytes 524288

commit v3 on v0

v3 whole, which is shorter than its diff:
```python
import math

import jax
import jax.numpy as jnp
from jax import lax
from jax.experimental import pallas as pl
from jax.experimental.pallas import tpu as pltpu
from jax.sharding import PartitionSpec as P

HD = 128
RUN = 64
NEG = -1e30
ROWS = 256
KEYS = 512
QUARTER = 16
LOG2E = math.log2(math.e)
MESH = pl.DeviceIdType.MESH

S_KV = 0
S_Q = 14
S_O = 16
S_STAT = 20
S_ATT = 24
S_FAR = 92
S_NEAR = 100
S_SIDE = 108
S_COUNT = 112


def device_at(x, y, core):
    return x * 8 + y * 2 + core


def kernel(
    q_hbm, k_hbm, v_hbm, w_hbm, out_ref,
    q_ref, v_ref, q_t, kv, s0, s1, p1, fade1, acc, mrow, lrow, o_send, s_send, o_recv, s_recv,
    att, w, prod, far, far_in, near, near_in, side, side_in, mine, fetched, send, recv,
):
    c, h = lax.axis_index("ctx"), lax.axis_index("head")
    x, y, core = c // 8, (c // 2) % 4, c % 2
    z, e = h // 2, h % 2
    scale = LOG2E / math.sqrt(HD)

    to_core = (device_at(x, y, 1 - core), h)
    to_up = (device_at(x, (y + 1) % 4, core), h)
    to_down = (device_at(x, (y + 3) % 4, core), h)
    to_x = (device_at(1 - x, y, core), h)
    to_zup = (c, ((z + 1) % 4) * 2 + e)
    to_zdown = (c, ((z + 3) % 4) * 2 + e)
    to_side = (c, z * 2 + 1 - e)
    partners = (to_core, to_up, to_down, to_x, to_zup, to_zdown, to_side)

    def remote(src, dst, number, where):
        return pltpu.make_async_remote_copy(
            src_ref=src, dst_ref=dst, send_sem=send.at[number], recv_sem=recv.at[number],
            device_id=where, device_id_type=MESH,
        )

    q_fetch = pltpu.make_async_copy(q_hbm, q_ref, fetched.at[0])
    v_fetch = pltpu.make_async_copy(v_hbm, v_ref, fetched.at[1])
    k_fetch = [
        pltpu.make_async_copy(
            k_hbm.at[pl.ds(i * KEYS, KEYS)], kv.at[i, pl.ds(0, KEYS)], fetched.at[2 + i]
        )
        for i in range(2)
    ]
    w_copy = pltpu.make_async_copy(w_hbm, w, fetched.at[4])
    for fetch in [q_fetch, v_fetch] + k_fetch:
        fetch.start()
    barrier = pltpu.get_barrier_semaphore()
    for partner in partners:
        pl.semaphore_signal(barrier, inc=1, device_id=partner, device_id_type=MESH)

    q_fetch.wait()
    for i in range(4):
        rows = slice(i * QUARTER, (i + 1) * QUARTER)
        heads = [q_ref[rows, j * HD : (j + 1) * HD] for j in range(16)]
        block = jnp.concatenate(heads, axis=0).astype(jnp.float32)
        q_t[i] = block.T.astype(jnp.bfloat16)
    v_fetch.wait()
    for half in range(2):
        for b in range(4):
            start = half * KEYS + b * HD
            piece = v_ref[start : start + HD].astype(jnp.float32)
            kv[half, KEYS + b * HD : KEYS + (b + 1) * HD] = piece.T.astype(jnp.bfloat16)
    for i in range(8):
        acc[i] = jnp.zeros((HD, ROWS), jnp.float32)
        mrow[i] = jnp.full((1, ROWS), NEG, jnp.float32)
        lrow[i] = jnp.zeros((1, ROWS), jnp.float32)

    for fetch in k_fetch:
        fetch.wait()
    w_copy.start()
    pl.semaphore_wait(barrier, len(partners))

    def kv_copy(number, source, target, where):
        return remote(kv.at[source], kv.at[target], S_KV + number, where)

    own_up = [kv_copy(0 + i, i, 12 + i, to_up) for i in range(2)]
    own_down = [kv_copy(2 + i, i, 4 + i, to_down) for i in range(2)]
    own_core = [kv_copy(4 + i, i, 2 + i, to_core) for i in range(2)]
    pass_12 = kv_copy(6, 12, 14, to_core)
    pass_4 = kv_copy(7, 4, 6, to_core)
    pass_13 = kv_copy(8, 13, 15, to_core)
    pass_5 = kv_copy(9, 5, 7, to_core)
    on_up = kv_copy(10, 12, 8, to_up)
    on_down = kv_copy(11, 5, 9, to_down)
    pass_8 = kv_copy(12, 8, 10, to_core)
    pass_9 = kv_copy(13, 9, 11, to_core)
    q_copy = [
        remote(q_t.at[pl.ds(2 * i, 2)], q_t.at[pl.ds(4 + 2 * i, 2)], S_Q + i, to_x)
        for i in range(2)
    ]
    o_copy = [remote(o_send.at[f], o_recv.at[f], S_O + f, to_x) for f in range(4)]
    s_copy = [remote(s_send.at[f], s_recv.at[f], S_STAT + f, to_x) for f in range(4)]

    own_up[0].start()
    own_down[0].start()
    for i in range(2):
        q_copy[i].start()
        own_core[i].start()

    def place(t):
        v = t % 8
        i = t % 4
        step = 12 - 8 * (i % 2) + 2 * (i // 2)
        late = jnp.where(v < 4, step + 1, 8 + i)
        slot = jnp.where(t < 16, i, jnp.where(t < 32, step, late))
        f = jnp.where(t < 32, t // 4 - 4, t // 8 - 4)
        one = jnp.where(t < 16, t // 4 * 2, f)
        two = jnp.where(t < 16, t // 4 * 2 + 1, f + 4)
        return slot, one, two

    def score(t, s_ref):
        slot, one, two = place(t)
        keys = kv[slot, 0:KEYS]
        for j, row in enumerate((one, two)):
            s_ref[:, j * ROWS : (j + 1) * ROWS] = (
                jnp.dot(keys, q_t[row], preferred_element_type=jnp.float32) * scale
            )

    def weigh(t, s_ref):
        slot, one, two = place(t)
        holder_core = jnp.where((slot // 2) % 2 == 1, 1 - core, core)
        holder = device_at(x, (y + slot // 4) % 4, holder_core)
        key_base = jnp.where(slot % 2 == 1, holder * RUN, -(1 << 20))
        token = lax.broadcasted_iota(jnp.int32, (RUN, ROWS), 1) % QUARTER
        key_token = lax.broadcasted_iota(jnp.int32, (RUN, ROWS), 0) - token
        rounded, fades = [], []
        for j, row in enumerate((one, two)):
            lanes = slice(j * ROWS, (j + 1) * ROWS)
            asker = device_at(jnp.where(row >= 4, 1 - x, x), y, core)
            limit = asker * RUN + (row % 4) * QUARTER - key_base
            tail = jnp.where(key_token <= limit, s_ref[KEYS - RUN :, lanes], NEG)
            scores = jnp.concatenate([s_ref[0 : KEYS - RUN, lanes], tail], axis=0)
            old = mrow[row]
            new = jnp.maximum(old, jnp.max(scores, axis=0, keepdims=True))
            weights = jnp.exp2(scores - new)
            fade = jnp.exp2(old - new)
            mrow[row] = new
            lrow[row] = lrow[row] * fade + jnp.sum(weights, axis=0, keepdims=True)
            rounded.append(weights.astype(jnp.bfloat16))
            fades.append(fade)
        return jnp.concatenate(rounded, axis=1), jnp.concatenate(fades, axis=1)

    def add_values(t, weights, fade):
        slot, one, two = place(t)
        values = jnp.concatenate(
            [kv[slot, KEYS + b * HD : KEYS + (b + 1) * HD] for b in range(4)], axis=1
        )
        for j, row in enumerate((one, two)):
            lanes = slice(j * ROWS, (j + 1) * ROWS)
            acc[row] = acc[row] * fade[:, lanes] + jnp.dot(
                values, weights[:, lanes], preferred_element_type=jnp.float32
            )

    def finish_neighbour(f):
        row = lax.broadcasted_iota(jnp.int32, (8, ROWS), 0)
        o_send[f] = (acc[4 + f] / lrow[4 + f]).astype(jnp.bfloat16)
        s_send[f] = jnp.where(row == 0, mrow[4 + f], lrow[4 + f])
        o_copy[f].start()
        s_copy[f].start()

    def combine(f):
        o_copy[f].wait_recv()
        s_copy[f].wait_recv()
        m_b, l_b = s_recv[f, 0:1], s_recv[f, 1:2]
        new = jnp.maximum(mrow[f], m_b)
        fade_a = jnp.exp2(mrow[f] - new)
        fade_b = jnp.exp2(m_b - new) * l_b
        summed = acc[f] * fade_a + o_recv[f].astype(jnp.float32) * fade_b
        done = (summed / (lrow[f] * fade_a + fade_b)).T.astype(jnp.bfloat16)
        for j in range(16):
            att[f, 0, :, j * HD : (j + 1) * HD] = done[j * QUARTER : (j + 1) * QUARTER]

    width = att.shape[3]

    def gather_copies(f):
        base = S_ATT + 17 * f

        def whole(number, source, target, where):
            return remote(att.at[f, source * 2], att.at[f, target * 2], base + number, where)

        def to_other_core(slot):
            return remote(att.at[f, slot * 2], att.at[f, slot * 2 + 1], base + slot, to_core)

        def part(number, source, target, piece, where):
            rows, lanes = pl.ds(0, QUARTER), pl.ds(piece * (width // 2), width // 2)
            return remote(
                att.at[f, source * 2, rows, lanes], att.at[f, target * 2, rows, lanes],
                base + number, where,
            )

        return dict(
            core=[to_other_core(slot) for slot in range(8)],
            x=[whole(8, 0, 4, to_x)],
            up=[whole(9, 0, 3, to_up), whole(10, 4, 7, to_up)],
            down=[whole(11, 0, 1, to_down), whole(12, 4, 5, to_down)],
            up2=[part(13, 3, 2, 0, to_up), part(14, 7, 6, 0, to_up)],
            down2=[part(15, 1, 2, 1, to_down), part(16, 5, 6, 1, to_down)],
        )

    gathers = [gather_copies(f) for f in range(4)]

    def gather_own(f):
        g = gathers[f]
        g["x"][0].start()
        g["up"][0].start()
        g["down"][0].start()
        g["core"][0].start()

    def gather_x(f):
        g = gathers[f]
        g["x"][0].wait_recv()
        g["up"][1].start()
        g["down"][1].start()
        g["core"][4].start()

    def gather_y(f, plane):
        g = gathers[f]
        g["up"][plane].wait_recv()
        g["up2"][plane].start()
        g["core"][plane * 4 + 3].start()
        g["down"][plane].wait_recv()
        g["down2"][plane].start()
        g["core"][plane * 4 + 1].start()

    def gather_y2(f, plane):
        g = gathers[f]
        g["up2"][plane].wait_recv()
        g["down2"][plane].wait_recv()
        g["core"][plane * 4 + 2].start()

    def gather_end(f):
        for slot in range(8):
            gathers[f]["core"][slot].wait_recv()

    cols = w.shape[1] // 2
    z_ways = (to_zup, to_zdown)
    far_copy = [
        [remote(far.at[f, i], far_in.at[f, i], S_FAR + f * 2 + i, z_ways[i]) for i in range(2)]
        for f in range(4)
    ]
    near_copy = [
        [remote(near.at[f, i], near_in.at[f, i], S_NEAR + f * 2 + i, z_ways[i]) for i in range(2)]
        for f in range(4)
    ]
    side_copy = [remote(side.at[f], side_in.at[f], S_SIDE + f, to_side) for f in range(4)]

    def product_of(f, distance, s, lanes):
        target = ((z + distance) % 4) * 2 + s
        slot = jnp.where(target // 4 == x, 0, 4) + (target % 4 - y + 4) % 4
        b = f % 2
        return jnp.concatenate(
            [prod[b, slot * 2 + core, :, lanes], prod[b, slot * 2 + 1 - core, :, lanes]], axis=0
        )

    span = 2 * QUARTER

    def reduce_far(f):
        block = att[f].reshape(16 * QUARTER, width)
        for way in range(2):
            lanes = slice(way * cols, (way + 1) * cols)
            prod[f % 2, :, :, lanes] = jnp.dot(
                block, w[:, lanes], preferred_element_type=jnp.float32
            ).reshape(16, QUARTER, cols)
            for s in range(2):
                far[f, way, s * span : (s + 1) * span] = product_of(f, 2, s, lanes).astype(
                    jnp.bfloat16
                )
            far_copy[f][way].start()

    def reduce_near(f):
        for way in range(2):
            other = slice((1 - way) * cols, (2 - way) * cols)
            lanes = slice(way * cols, (way + 1) * cols)
            far_copy[f][way].wait_recv()
            for s in range(2):
                rows = slice(s * span, (s + 1) * span)
                near[f, way, rows, other] = product_of(f, 1 + 2 * way, s, other).astype(
                    jnp.bfloat16
                )
                near[f, way, rows, lanes] = (
                    product_of(f, 1 + 2 * way, s, lanes) + far_in[f, way, rows].astype(jnp.float32)
                ).astype(jnp.bfloat16)
            near_copy[f][way].start()

    def reduce_last(f):
        near_copy[f][0].wait_recv()
        near_copy[f][1].wait_recv()

        def summed(s):
            rows = pl.ds(pl.multiple_of(s * span, span), span)
            return (
                product_of(f, 0, s, slice(0, 2 * cols))
                + near_in[f, 0, rows].astype(jnp.float32)
                + near_in[f, 1, rows].astype(jnp.float32)
            )

        side[f] = summed(1 - e).astype(jnp.bfloat16)
        side_copy[f].start()
        mine[f] = summed(e)

    def reduce_end(f):
        side_copy[f].wait_recv()
        done = (mine[f] + side_in[f].astype(jnp.float32)).astype(jnp.bfloat16)
        for i in range(2):
            start = i * RUN + f * QUARTER
            out_ref[start : start + QUARTER] = done[i * QUARTER : (i + 1) * QUARTER]

    def wait_all(*copies):
        for copy in copies:
            copy.wait_recv()

    def pass_on(arrived, *onward):
        arrived.wait_recv()
        for copy in onward:
            copy.start()

    def start_rest():
        wait_all(*own_core)
        own_up[1].start()
        own_down[1].start()

    before = [
        (0, start_rest),
        (3, lambda: wait_all(*q_copy)),
        (7, lambda: pass_on(own_up[0], on_up, pass_12)),
        (7, lambda: pass_on(own_down[0], pass_4)),
        (8, lambda: wait_all(pass_12, pass_4)),
        (13, lambda: pass_on(own_down[1], on_down, pass_5)),
        (13, lambda: pass_on(own_up[1], pass_13)),
        (16, lambda: wait_all(pass_13, pass_5)),
        (17, lambda: pass_on(on_up, pass_8)),
        (17, lambda: pass_on(on_down, pass_9)),
        (18, lambda: wait_all(pass_8, pass_9)),
        (28, w_copy.wait),
    ]
    after = [(20 + 4 * f, lambda f=f: finish_neighbour(f)) for f in range(4)]
    for f in range(4):
        after += [
            (22 + 4 * f, lambda f=f: combine(f)),
            (22 + 4 * f, lambda f=f: gather_own(f)),
            (24 + 4 * f, lambda f=f: gather_x(f)),
            (24 + 4 * f, lambda f=f: gather_y(f, 0)),
            (26 + 4 * f, lambda f=f: gather_y(f, 1)),
            (26 + 4 * f, lambda f=f: gather_y2(f, 0)),
            (28 + 4 * f, lambda f=f: gather_y2(f, 1)),
            (29 + 4 * f, lambda f=f: gather_end(f)),
            (29 + 4 * f, lambda f=f: reduce_far(f)),
            (31 + 4 * f, lambda f=f: reduce_near(f)),
            (33 + 4 * f, lambda f=f: reduce_last(f)),
            (35 + 4 * f, lambda f=f: reduce_end(f)),
        ]
    after.sort(key=lambda item: item[0])

    def run(events, u):
        for k in sorted({step for step, _ in events}):

            @pl.when(u == k)
            def _():
                for step, action in events:
                    if step == k:
                        action()

    def unit(u, carry):
        run(before, u)
        t = 2 * u
        score(t + 1, s1)
        weights, fade = weigh(t, s0)
        add_values(jnp.maximum(t - 1, 0), p1[...], fade1[...])
        score(jnp.minimum(t + 2, 63), s0)
        weights_1, fade_1 = weigh(t + 1, s1)
        add_values(t, weights, fade)
        p1[...] = weights_1
        fade1[...] = fade_1
        run([(step, action) for step, action in after if step < 32], u)
        return carry

    p1[...] = jnp.zeros_like(p1)
    fade1[...] = jnp.ones_like(fade1)
    score(0, s0)
    lax.fori_loop(0, 32, unit, 0)
    add_values(63, p1[...], fade1[...])
    for step, action in after:
        if step >= 32:
            action()

    sent = own_up + own_down + own_core + [pass_12, pass_4, pass_13, pass_5, on_up, on_down]
    sent += [pass_8, pass_9] + q_copy + o_copy + s_copy + side_copy
    for f in range(4):
        for copies in gathers[f].values():
            sent += copies
        sent += far_copy[f] + near_copy[f]
    for copy in sent:
        copy.wait_send()


def body(queries, key_cache, value_cache, out_weight):
    tokens, width = queries.shape
    cols = out_weight.shape[1]
    vmem, anywhere = pl.BlockSpec(memory_space=pltpu.VMEM), pl.BlockSpec(memory_space=pl.ANY)
    bf16, f32 = jnp.bfloat16, jnp.float32
    return pl.pallas_call(
        kernel,
        out_shape=jax.ShapeDtypeStruct((2 * tokens, cols), bf16),
        in_specs=[anywhere] * 4,
        out_specs=vmem,
        scratch_shapes=[
            pltpu.VMEM(queries.shape, bf16),
            pltpu.VMEM(value_cache.shape, bf16),
            pltpu.VMEM((8, HD, ROWS), bf16),
            pltpu.VMEM((16, 2 * KEYS, HD), bf16),
            pltpu.VMEM((KEYS, 2 * ROWS), f32),
            pltpu.VMEM((KEYS, 2 * ROWS), f32),
            pltpu.VMEM((KEYS, 2 * ROWS), bf16),
            pltpu.VMEM((1, 2 * ROWS), f32),
            pltpu.VMEM((8, HD, ROWS), f32),
            pltpu.VMEM((8, 1, ROWS), f32),
            pltpu.VMEM((8, 1, ROWS), f32),
            pltpu.VMEM((4, HD, ROWS), bf16),
            pltpu.VMEM((4, 8, ROWS), f32),
            pltpu.VMEM((4, HD, ROWS), bf16),
            pltpu.VMEM((4, 8, ROWS), f32),
            pltpu.VMEM((4, 16, QUARTER, width), bf16),
            pltpu.VMEM(out_weight.shape, bf16),
            pltpu.VMEM((2, 16, QUARTER, cols), f32),
            pltpu.VMEM((4, 2, tokens, cols // 2), bf16),
            pltpu.VMEM((4, 2, tokens, cols // 2), bf16),
            pltpu.VMEM((4, 2, tokens, cols), bf16),
            pltpu.VMEM((4, 2, tokens, cols), bf16),
            pltpu.VMEM((4, 2 * QUARTER, cols), bf16),
            pltpu.VMEM((4, 2 * QUARTER, cols), bf16),
            pltpu.VMEM((4, 2 * QUARTER, cols), f32),
            pltpu.SemaphoreType.DMA((5,)),
            pltpu.SemaphoreType.DMA((S_COUNT,)),
            pltpu.SemaphoreType.DMA((S_COUNT,)),
        ],
        compiler_params=pltpu.CompilerParams(
            collective_id=0, has_side_effects=True, vmem_limit_bytes=56 * 1024 * 1024
        ),
        cost_estimate=pl.CostEstimate(
            flops=13_000_000_000, bytes_accessed=5_000_000, transcendentals=17_000_000
        ),
    )(queries, key_cache, value_cache, out_weight)


def solution(mesh):
    in_specs = (P("ctx", "head"), P("ctx", "head"), P("ctx", "head"), P("head", "ctx"))
    out_specs = P("head", "ctx")
    return jax.shard_map(body, mesh=mesh, in_specs=in_specs, out_specs=out_specs, check_vma=False)
```

time: 453 us -> 100 us (0.22)
  waiting for transfers between devices: 333 us -> 0 us
  Pallas kernels: 0 us -> 98.6 us
  matrix products: 58.4 us -> 0 us
  other arithmetic: 32.3 us -> 0 us
  between operations: 13.4 us -> 0.01 us
  starting transfers between devices: 9.16 us -> 0 us
    ppermute x64 -> x0, waiting for transfers between devices: 211 us -> none  [passed_along(): return lax.ppermute(value, axis, pairs)]
    pallas_call x0 -> x1, Pallas kernels: none -> 98.6 us  [body(): pl.pallas_call(kernel, out_shape=jax.ShapeDtypeStruct((2 * tokens, cols),...]
    reduce_scatter x1 -> x0, waiting for transfers between devices: 84.9 us -> none  [body(): lax.psum_scatter(terms, 'head', scatter_dimension=0, tiled=True)]
    dot_general x33 -> x0, matrix products: 58.4 us -> none  [the longest x16 29.9 us: attend(): jnp.einsum('tkgd,ckd->tkgc', grouped, key_view, preferred_element_type=jn...]
    all_gather x1 -> x0, waiting for transfers between devices: 37.3 us -> none  [body(): lax.all_gather(attended, 'ctx', axis=0, tiled=True)]
    reduce_sum x16 -> x0, other arithmetic: 21.4 us -> none  [attend(): weight_sum = jnp.sum(weights, axis=-1)]
    ppermute x64 -> x0, starting transfers between devices: 9.12 us -> none  [passed_along(): return lax.ppermute(value, axis, pairs)]
    add x64 -> x0, other arithmetic: 7.22 us -> none  [the longest x16 6.56 us: combine(): summed_a * scale_a[..., None] + summed_b * scale_b[..., None]]
  transfers between devices with their start and end apart: 66 -> 0, of which waited for: 34 -> 0; matrix products, arithmetic and copies ran while one was open for 0% -> 0% of each run, Pallas kernels for 0% -> 0%
where the time goes in v3:
time: 100 us
  Pallas kernels  98.6 us (99%)
  local copies, waits for them, and re-layouts  1.67 us (2%)
    pallas_call x1, Pallas kernels, body(): pl.pallas_call(kernel, out_shape=jax.ShapeDtypeStruct((2 * tokens, cols),...  98.6 us

profile of v3, /device:TPU:0, one launch (start us, length us, event | category | flops | bytes accessed | tf_op | source)
XLA Modules:
  0.0 100.3 jit_solution(7479493604081219124)
XLA Ops:
  0.0 98.6 %shard_map.46 = bf16[128,1024]{1,0:T(8,128)(2,1)} custom-call(bf16[64,2048]{1,0:T(8,128)(2,1)} %q_hbm.1, bf16[1024,128]{1,0:T(8,128)(2,1)} %k_hbm.1, bf16[1024,128]{1,0:T(8,128)(2,1)} %v_hbm.1, bf16[2048,1024]{1,0:T(8,128)(2,1)} %w_hbm.1), custom_call_target="tpu_custom_call" | custom-call | flops 12999999488 | bytes 5000000 | tf_op jit(solution)/shard_map/pallas_call | solution.py:424
  98.6 1.7 %copy.6 = bf16[128,1024]{1,0:T(8,128)(2,1)} copy(bf16[128,1024]{1,0:T(8,128)(2,1)} %shard_map.46) | data formatting | bytes 524288

commit v4 on v0

v4 whole, which is shorter than its diff:
```python
import math

import jax
import jax.numpy as jnp
from jax import lax
from jax.experimental import pallas as pl
from jax.experimental.pallas import tpu as pltpu
from jax.sharding import PartitionSpec as P

HD = 128
RUN = 64
NEG = -1e30
ROWS = 512
HALF = 32
KEYS = 512
LOG2E = math.log2(math.e)
MESH = pl.DeviceIdType.MESH

S_KV = 0
S_Q = 14
S_O = 16
S_STAT = 18
S_ATT = 20
S_FAR = 54
S_PLAIN = 58
S_LATER = 62
S_SIDE = 66
S_COUNT = 68


def device_at(x, y, core):
    return x * 8 + y * 2 + core


def kernel(
    q_hbm, k_hbm, v_hbm, w_hbm, out_ref,
    q_ref, k_ref, q_s, kv, s0, s1, p1, fade1, acc, mrow, o_send, s_send, o_recv, s_recv,
    att, w, terms, far_in, plain_in, added, added_in, side, side_in, mine, fetched, send, recv,
):
    c, h = lax.axis_index("ctx"), lax.axis_index("head")
    x, y, core = c // 8, (c // 2) % 4, c % 2
    z, e = h // 2, h % 2
    scale = LOG2E / math.sqrt(HD)

    to_core = (device_at(x, y, 1 - core), h)
    to_up = (device_at(x, (y + 1) % 4, core), h)
    to_down = (device_at(x, (y + 3) % 4, core), h)
    to_x = (device_at(1 - x, y, core), h)
    z_ways = ((c, ((z + 1) % 4) * 2 + e), (c, ((z + 3) % 4) * 2 + e))
    to_side = (c, z * 2 + 1 - e)
    partners = (to_core, to_up, to_down, to_x, to_side) + z_ways

    def remote(src, dst, number, where):
        return pltpu.make_async_remote_copy(
            src_ref=src, dst_ref=dst, send_sem=send.at[number], recv_sem=recv.at[number],
            device_id=where, device_id_type=MESH,
        )

    q_fetch = pltpu.make_async_copy(q_hbm, q_ref, fetched.at[0])
    k_fetch = pltpu.make_async_copy(k_hbm, k_ref, fetched.at[1])
    v_fetch = [
        pltpu.make_async_copy(
            v_hbm.at[pl.ds(i * KEYS, KEYS)], kv.at[i, pl.ds(0, KEYS)], fetched.at[2 + i]
        )
        for i in range(2)
    ]
    w_copy = pltpu.make_async_copy(w_hbm, w, fetched.at[4])
    for fetch in [k_fetch, q_fetch] + v_fetch:
        fetch.start()
    barrier = pltpu.get_barrier_semaphore()
    for partner in partners:
        pl.semaphore_signal(barrier, inc=1, device_id=partner, device_id_type=MESH)

    k_fetch.wait()
    for half in range(2):
        for b in range(4):
            start = half * KEYS + b * HD
            piece = k_ref[start : start + HD].astype(jnp.float32)
            kv[half, KEYS + b * HD : KEYS + (b + 1) * HD] = piece.T.astype(jnp.bfloat16)
    q_fetch.wait()
    for r in range(2):
        for i in range(16):
            q_s[r, i * HALF : (i + 1) * HALF] = q_ref[
                r * HALF : (r + 1) * HALF, i * HD : (i + 1) * HD
            ]
    for fetch in v_fetch:
        fetch.wait()
    w_copy.start()
    pl.semaphore_wait(barrier, len(partners))

    def kv_copy(number, source, target, where):
        return remote(kv.at[source], kv.at[target], S_KV + number, where)

    own_up = [kv_copy(0 + i, i, 12 + i, to_up) for i in range(2)]
    own_down = [kv_copy(2 + i, i, 4 + i, to_down) for i in range(2)]
    own_core = [kv_copy(4 + i, i, 2 + i, to_core) for i in range(2)]
    pass_12 = kv_copy(6, 12, 14, to_core)
    pass_4 = kv_copy(7, 4, 6, to_core)
    pass_13 = kv_copy(8, 13, 15, to_core)
    pass_5 = kv_copy(9, 5, 7, to_core)
    on_up = kv_copy(10, 12, 8, to_up)
    on_down = kv_copy(11, 5, 9, to_down)
    pass_8 = kv_copy(12, 8, 10, to_core)
    pass_9 = kv_copy(13, 9, 11, to_core)
    q_copy = [remote(q_s.at[i], q_s.at[2 + i], S_Q + i, to_x) for i in range(2)]
    o_copy = [remote(o_send.at[f], o_recv.at[f], S_O + f, to_x) for f in range(2)]
    s_copy = [remote(s_send.at[f], s_recv.at[f], S_STAT + f, to_x) for f in range(2)]

    for i in range(2):
        own_core[i].start()
    q_copy[0].start()
    own_up[0].start()
    own_down[0].start()
    q_copy[1].start()
    for r in range(4):
        acc[r] = jnp.zeros((ROWS, 2 * HD), jnp.float32)
        mrow[r] = jnp.full((ROWS, HD), NEG, jnp.float32)

    def place(t):
        v = (t - 16) % 8
        f = (t - 16) // 8
        pair = jnp.where(t < 8, t // 2 % 2, jnp.where(t < 16, t // 4, 4 + v // 2))
        pair = jnp.where((t >= 16) & (v >= 4), 6 + v % 2, pair)
        row = jnp.where(t < 8, t // 4 * 2 + t % 2, jnp.where(t < 16, t % 4, v % 2 * 2 + f))
        row = jnp.where((t >= 16) & (v >= 4), (1 - (v - 4) // 2) * 2 + f, row)
        i = pair - 2
        middle = 12 + 2 * (i % 2) + i // 2
        one = jnp.where(pair < 2, 2 * pair, jnp.where(pair < 6, middle, 2 * pair - 4))
        two = jnp.where((pair >= 2) & (pair < 6), one - 8, one + 1)
        return one, two, row

    def score(t, s_ref):
        one, two, row = place(t)
        queries = q_s[row]
        for j, slot in enumerate((one, two)):
            keys = jnp.concatenate(
                [kv[slot, KEYS + b * HD : KEYS + (b + 1) * HD] for b in range(4)], axis=1
            )
            s_ref[:, j * KEYS : (j + 1) * KEYS] = (
                jnp.dot(queries, keys, preferred_element_type=jnp.float32) * scale
            )

    def weigh(t, s_ref):
        one, two, row = place(t)
        asker = device_at(jnp.where(row >= 2, 1 - x, x), y, core)
        token = lax.broadcasted_iota(jnp.int32, (ROWS, HD), 0) % HALF
        key_token = lax.broadcasted_iota(jnp.int32, (ROWS, HD), 1) - RUN
        pieces = []
        for j, slot in enumerate((one, two)):
            holder_core = jnp.where((slot // 2) % 2 == 1, 1 - core, core)
            holder = device_at(x, (y + slot // 4) % 4, holder_core)
            first = jnp.where(slot % 2 == 1, holder * RUN, -(1 << 20))
            limit = asker * RUN + (row % 2) * HALF - first
            end = (j + 1) * KEYS
            seen = (key_token < 0) | (key_token - token <= limit)
            pieces.append(s_ref[:, j * KEYS : end - HD])
            pieces.append(jnp.where(seen, s_ref[:, end - HD : end], NEG))
        scores = jnp.concatenate(pieces, axis=1)
        old = mrow[row]
        new = jnp.maximum(old, jnp.max(scores, axis=1, keepdims=True))
        weights = jnp.exp2(scores - jnp.concatenate([new] * (2 * KEYS // HD), axis=1))
        mrow[row] = new
        return weights.astype(jnp.bfloat16), jnp.exp2(old - new)

    def add_values(t, weights, fade):
        one, two, row = place(t)
        ones = jnp.ones((KEYS, HD), jnp.bfloat16)
        values = jnp.concatenate(
            [jnp.concatenate([kv[slot, 0:KEYS], ones], axis=1) for slot in (one, two)], axis=0
        )
        acc[row] = acc[row] * jnp.concatenate([fade, fade], axis=1) + jnp.dot(
            weights, values, preferred_element_type=jnp.float32
        )

    def normalised(row):
        total = acc[row, :, HD : 2 * HD]
        return acc[row, :, 0:HD] / total, mrow[row] + jnp.log(total) * LOG2E

    def finish_neighbour(f):
        value, level = normalised(2 + f)
        o_send[f] = value.astype(jnp.bfloat16)
        s_send[f] = level.T[0:8]
        o_copy[f].start()
        s_copy[f].start()

    def block_of(owner):
        start = owner * HALF
        return start if isinstance(start, int) else pl.multiple_of(start, HALF)

    def combine(f):
        value, level = normalised(f)
        o_copy[f].wait_recv()
        s_copy[f].wait_recv()
        other = jnp.broadcast_to(s_recv[f, 0:1], (HD, ROWS)).T
        top = jnp.maximum(level, other)
        part_a, part_b = jnp.exp2(level - top), jnp.exp2(other - top)
        done = (value * part_a + o_recv[f].astype(jnp.float32) * part_b) / (part_a + part_b)
        done = done.astype(jnp.bfloat16)
        for i in range(16):
            att[f, pl.ds(block_of(c), HALF), i * HD : (i + 1) * HD] = done[
                i * HALF : (i + 1) * HALF
            ]

    def gather_copy(f, number, dx, dy, where, part=None, from_core=None):
        owner = device_at(1 - x if dx else x, (y + dy) % 4, core if from_core is None else from_core)
        start, size = block_of(owner), HALF
        if part is not None:
            size = HALF // 2
            start = pl.multiple_of(start + part * size, size)
        block = att.at[f, pl.ds(start, size)]
        return remote(block, block, S_ATT + 17 * f + number, where)

    sent = own_up + own_down + own_core + [pass_12, pass_4, pass_13, pass_5, on_up, on_down]
    sent += [pass_8, pass_9] + q_copy + o_copy + s_copy

    def arrived(f, number, dx, dy, part=None, from_core=None):
        gather_copy(f, number, dx, dy, to_core, part, from_core).wait_recv()

    def gather_start(f, *args):
        gather_copy(f, *args).start()

    def gather_own(f):
        gather_start(f, 8, 0, 0, to_x)
        gather_start(f, 9, 0, 0, to_up)
        gather_start(f, 11, 0, 0, to_down)
        gather_start(f, 0, 0, 0, to_core)

    def gather_x(f):
        arrived(f, 8, 1, 0)
        gather_start(f, 10, 1, 0, to_up)
        gather_start(f, 12, 1, 0, to_down)
        gather_start(f, 4, 1, 0, to_core)

    def gather_y(f, plane):
        arrived(f, 9 + plane, plane, 3)
        gather_start(f, 13 + plane, plane, 3, to_up, 0)
        gather_start(f, 4 * plane + 3, plane, 3, to_core)
        arrived(f, 11 + plane, plane, 1)
        gather_start(f, 15 + plane, plane, 1, to_down, 1)
        gather_start(f, 4 * plane + 1, plane, 1, to_core)

    def gather_y2(f, plane):
        arrived(f, 13 + plane, plane, 2, 0)
        arrived(f, 15 + plane, plane, 2, 1)
        gather_start(f, 4 * plane + 2, plane, 2, to_core)

    def gather_end(f):
        for plane in range(2):
            for dy in range(4):
                arrived(f, 4 * plane + dy, plane, dy, None, 1 - core)

    def gather_sent(f):
        copies = [gather_copy(f, 8, 0, 0, to_x)]
        for plane in range(2):
            copies += [gather_copy(f, 4 * plane + dy, plane, dy, to_core) for dy in range(4)]
            copies += [gather_copy(f, 9 + plane, plane, 0, to_up)]
            copies += [gather_copy(f, 11 + plane, plane, 0, to_down)]
            copies += [gather_copy(f, 13 + plane, plane, 3, to_up, 0)]
            copies += [gather_copy(f, 15 + plane, plane, 1, to_down, 1)]
        return copies

    cols = w.shape[1] // 2
    rows = 4 * HALF

    def half(i):
        return pl.ds(i * cols, cols)

    def block(distance):
        return pl.ds(pl.multiple_of(((z + distance) % 4) * rows, rows), rows)

    far_copy = [
        [
            remote(terms.at[f, block(2), half(i)], far_in.at[f, i], S_FAR + 2 * f + i, z_ways[i])
            for i in range(2)
        ]
        for f in range(2)
    ]
    plain_copy = [
        [
            remote(
                terms.at[f, block(1 + 2 * i), half(1 - i)], plain_in.at[f, i],
                S_PLAIN + 2 * f + i, z_ways[i],
            )
            for i in range(2)
        ]
        for f in range(2)
    ]
    later_copy = [
        [
            remote(added.at[f, i], added_in.at[f, i], S_LATER + 2 * f + i, z_ways[i])
            for i in range(2)
        ]
        for f in range(2)
    ]
    side_copy = [remote(side.at[f], side_in.at[f], S_SIDE + f, to_side) for f in range(2)]

    def project(f):
        for i in range(2):
            terms[f, :, half(i)] = jnp.dot(
                att[f], w[:, half(i)], preferred_element_type=jnp.float32
            ).astype(jnp.bfloat16)
            far_copy[f][i].start()
        for i in range(2):
            plain_copy[f][i].start()

    def reduce_added(f):
        for i in range(2):
            far_copy[f][i].wait_recv()
            added[f, i] = (
                terms[f, block(1 + 2 * i), half(i)].astype(jnp.float32)
                + far_in[f, i].astype(jnp.float32)
            ).astype(jnp.bfloat16)
            later_copy[f][i].start()

    def reduce_last(f):
        for i in range(2):
            plain_copy[f][i].wait_recv()
        for i in range(2):
            later_copy[f][i].wait_recv()

        def summed(s, i):
            size = rows // 2
            part = pl.ds(pl.multiple_of(s * size, size), size)
            own = pl.ds(pl.multiple_of(z * rows + s * size, size), size)
            return (
                terms[f, own, half(i)].astype(jnp.float32)
                + added_in[f, i, part].astype(jnp.float32)
                + plain_in[f, 1 - i, part].astype(jnp.float32)
            )

        for i in range(2):
            side[f, :, half(i)] = summed(1 - e, i).astype(jnp.bfloat16)
        side_copy[f].start()
        for i in range(2):
            mine[f, :, half(i)] = summed(e, i)

    def reduce_end(f):
        side_copy[f].wait_recv()
        done = (mine[f] + side_in[f].astype(jnp.float32)).astype(jnp.bfloat16)
        for i in range(2):
            start = i * RUN + f * HALF
            out_ref[start : start + HALF] = done[i * HALF : (i + 1) * HALF]

    def wait_all(*copies):
        for copy in copies:
            copy.wait_recv()

    def pass_on(arrival, *onward):
        arrival.wait_recv()
        for copy in onward:
            copy.start()

    def start_rest():
        wait_all(*own_core)
        own_up[1].start()
        own_down[1].start()

    before = [
        (0, start_rest),
        (1, lambda: wait_all(q_copy[0])),
        (2, lambda: wait_all(q_copy[1])),
        (3, lambda: pass_on(own_up[0], on_up, pass_12)),
        (3, lambda: pass_on(own_down[0], pass_4)),
        (5, lambda: wait_all(pass_12, pass_4)),
        (7, lambda: pass_on(own_down[1], on_down, pass_5)),
        (7, lambda: pass_on(own_up[1], pass_13)),
        (8, lambda: wait_all(pass_13, pass_5)),
        (9, lambda: pass_on(on_up, pass_8)),
        (9, lambda: pass_on(on_down, pass_9)),
        (10, lambda: wait_all(pass_8, pass_9)),
    ]
    after = [
        (11, lambda: finish_neighbour(0)),
        (13, lambda: combine(0)),
        (13, lambda: gather_own(0)),
        (15, lambda: finish_neighbour(1)),
        (15, lambda: gather_x(0)),
    ]

    def run(events, u):
        for k in sorted({step for step, _ in events}):

            @pl.when(u == k)
            def _():
                for step, action in events:
                    if step == k:
                        action()

    def unit(u, carry):
        run(before, u)
        t = 2 * u
        score(t + 1, s1)
        weights, fade = weigh(t, s0)
        add_values(jnp.maximum(t - 1, 0), p1[...], fade1[...])
        score(jnp.minimum(t + 2, 31), s0)
        weights_1, fade_1 = weigh(t + 1, s1)
        add_values(t, weights, fade)
        p1[...] = weights_1
        fade1[...] = fade_1
        run(after, u)
        return carry

    p1[...] = jnp.zeros_like(p1)
    fade1[...] = jnp.ones_like(fade1)
    score(0, s0)
    lax.fori_loop(0, 16, unit, 0)
    gather_y(0, 0)
    add_values(31, p1[...], fade1[...])
    gather_y(0, 1)
    combine(1)
    gather_own(1)
    gather_y2(0, 0)
    gather_y2(0, 1)
    gather_x(1)
    w_copy.wait()
    gather_end(0)
    project(0)
    gather_y(1, 0)
    gather_y(1, 1)
    reduce_added(0)
    gather_y2(1, 0)
    gather_y2(1, 1)
    gather_end(1)
    project(1)
    reduce_last(0)
    reduce_added(1)
    reduce_end(0)
    reduce_last(1)
    reduce_end(1)

    sent += side_copy
    for f in range(2):
        sent += gather_sent(f) + far_copy[f] + plain_copy[f] + later_copy[f]
    for copy in sent:
        copy.wait_send()


def body(queries, key_cache, value_cache, out_weight):
    tokens, width = queries.shape
    cols = out_weight.shape[1]
    all_rows = tokens // 2 * lax.axis_size("ctx")
    vmem, anywhere = pl.BlockSpec(memory_space=pltpu.VMEM), pl.BlockSpec(memory_space=pl.ANY)
    bf16, f32 = jnp.bfloat16, jnp.float32
    piece = pltpu.VMEM((2, 2, 2 * tokens, cols // 2), bf16)
    return pl.pallas_call(
        kernel,
        out_shape=jax.ShapeDtypeStruct((2 * tokens, cols), bf16),
        in_specs=[anywhere] * 4,
        out_specs=vmem,
        scratch_shapes=[
            pltpu.VMEM(queries.shape, bf16),
            pltpu.VMEM(key_cache.shape, bf16),
            pltpu.VMEM((4, ROWS, HD), bf16),
            pltpu.VMEM((16, 2 * KEYS, HD), bf16),
            pltpu.VMEM((ROWS, 2 * KEYS), f32),
            pltpu.VMEM((ROWS, 2 * KEYS), f32),
            pltpu.VMEM((ROWS, 2 * KEYS), bf16),
            pltpu.VMEM((ROWS, HD), f32),
            pltpu.VMEM((4, ROWS, 2 * HD), f32),
            pltpu.VMEM((4, ROWS, HD), f32),
            pltpu.VMEM((2, ROWS, HD), bf16),
            pltpu.VMEM((2, 8, ROWS), f32),
            pltpu.VMEM((2, ROWS, HD), bf16),
            pltpu.VMEM((2, 8, ROWS), f32),
            pltpu.VMEM((2, all_rows, width), bf16),
            pltpu.VMEM(out_weight.shape, bf16),
            pltpu.VMEM((2, all_rows, cols), bf16),
            piece,
            piece,
            piece,
            piece,
            pltpu.VMEM((2, tokens, cols), bf16),
            pltpu.VMEM((2, tokens, cols), bf16),
            pltpu.VMEM((2, tokens, cols), f32),
            pltpu.SemaphoreType.DMA((5,)),
            pltpu.SemaphoreType.DMA((S_COUNT,)),
            pltpu.SemaphoreType.DMA((S_COUNT,)),
        ],
        compiler_params=pltpu.CompilerParams(
            collective_id=0, has_side_effects=True, vmem_limit_bytes=56 * 1024 * 1024
        ),
        cost_estimate=pl.CostEstimate(
            flops=13_000_000_000, bytes_accessed=5_000_000, transcendentals=17_000_000
        ),
    )(queries, key_cache, value_cache, out_weight)


def solution(mesh):
    in_specs = (P("ctx", "head"), P("ctx", "head"), P("ctx", "head"), P("head", "ctx"))
    out_specs = P("head", "ctx")
    return jax.shard_map(body, mesh=mesh, in_specs=in_specs, out_specs=out_specs, check_vma=False)
```

time: 453 us -> 85 us (0.19)
  waiting for transfers between devices: 333 us -> 0 us
  Pallas kernels: 0 us -> 83.1 us
  matrix products: 58.4 us -> 0 us
  other arithmetic: 32.3 us -> 0 us
  between operations: 13.4 us -> 0.01 us
  starting transfers between devices: 9.16 us -> 0 us
    ppermute x64 -> x0, waiting for transfers between devices: 211 us -> none  [passed_along(): return lax.ppermute(value, axis, pairs)]
    reduce_scatter x1 -> x0, waiting for transfers between devices: 84.9 us -> none  [body(): lax.psum_scatter(terms, 'head', scatter_dimension=0, tiled=True)]
    pallas_call x0 -> x1, Pallas kernels: none -> 83.1 us  [body(): pl.pallas_call(kernel, out_shape=jax.ShapeDtypeStruct((2 * tokens, cols),...]
    dot_general x33 -> x0, matrix products: 58.4 us -> none  [the longest x16 29.9 us: attend(): jnp.einsum('tkgd,ckd->tkgc', grouped, key_view, preferred_element_type=jn...]
    all_gather x1 -> x0, waiting for transfers between devices: 37.3 us -> none  [body(): lax.all_gather(attended, 'ctx', axis=0, tiled=True)]
    reduce_sum x16 -> x0, other arithmetic: 21.4 us -> none  [attend(): weight_sum = jnp.sum(weights, axis=-1)]
    ppermute x64 -> x0, starting transfers between devices: 9.12 us -> none  [passed_along(): return lax.ppermute(value, axis, pairs)]
    add x64 -> x0, other arithmetic: 7.22 us -> none  [the longest x16 6.56 us: combine(): summed_a * scale_a[..., None] + summed_b * scale_b[..., None]]
  transfers between devices with their start and end apart: 66 -> 0, of which waited for: 34 -> 0; matrix products, arithmetic and copies ran while one was open for 0% -> 0% of each run, Pallas kernels for 0% -> 0%
where the time goes in v4:
time: 85 us; the launch traced here: 84.7 us
  Pallas kernels  83.1 us (98%)
  local copies, waits for them, and re-layouts  1.67 us (2%)
    pallas_call x1, Pallas kernels, body(): pl.pallas_call(kernel, out_shape=jax.ShapeDtypeStruct((2 * tokens, cols),...  83.1 us

profile of v4, /device:TPU:0, one launch (start us, length us, event | category | flops | bytes accessed | tf_op | source)
XLA Modules:
  0.0 84.7 jit_solution(11735843952462297617)
XLA Ops:
  0.0 83.1 %shard_map.46 = bf16[128,1024]{1,0:T(8,128)(2,1)} custom-call(bf16[64,2048]{1,0:T(8,128)(2,1)} %q_hbm.1, bf16[1024,128]{1,0:T(8,128)(2,1)} %k_hbm.1, bf16[1024,128]{1,0:T(8,128)(2,1)} %v_hbm.1, bf16[2048,1024]{1,0:T(8,128)(2,1)} %w_hbm.1), custom_call_target="tpu_custom_call" | custom-call | flops 12999999488 | bytes 5000000 | tf_op jit(solution)/shard_map/pallas_call | solution.py:445
  83.1 1.7 %copy.6 = bf16[128,1024]{1,0:T(8,128)(2,1)} copy(bf16[128,1024]{1,0:T(8,128)(2,1)} %shard_map.46) | data formatting | bytes 524288

commit v5 on v4

--- a/solution.py
+++ b/solution.py
@@ -117,12 +117,10 @@
         mrow[r] = jnp.full((ROWS, HD), NEG, jnp.float32)
 
     def place(t):
-        v = (t - 16) % 8
-        f = (t - 16) // 8
-        pair = jnp.where(t < 8, t // 2 % 2, jnp.where(t < 16, t // 4, 4 + v // 2))
-        pair = jnp.where((t >= 16) & (v >= 4), 6 + v % 2, pair)
-        row = jnp.where(t < 8, t // 4 * 2 + t % 2, jnp.where(t < 16, t % 4, v % 2 * 2 + f))
-        row = jnp.where((t >= 16) & (v >= 4), (1 - (v - 4) // 2) * 2 + f, row)
+        f, q = (t - 8) // 12, (t - 8) % 12
+        pair = jnp.where(t < 8, t // 2 % 2, jnp.where(q < 8, 2 + q // 2, 6 + q % 2))
+        late = jnp.where(q < 8, q % 2, 1 - (q - 8) // 2) * 2 + f
+        row = jnp.where(t < 8, t // 4 * 2 + t % 2, late)
         i = pair - 2
         middle = 12 + 2 * (i % 2) + i // 2
         one = jnp.where(pair < 2, 2 * pair, jnp.where(pair < 6, middle, 2 * pair - 4))
@@ -361,20 +359,23 @@
         (2, lambda: wait_all(q_copy[1])),
         (3, lambda: pass_on(own_up[0], on_up, pass_12)),
         (3, lambda: pass_on(own_down[0], pass_4)),
-        (5, lambda: wait_all(pass_12, pass_4)),
-        (7, lambda: pass_on(own_down[1], on_down, pass_5)),
-        (7, lambda: pass_on(own_up[1], pass_13)),
-        (8, lambda: wait_all(pass_13, pass_5)),
-        (9, lambda: pass_on(on_up, pass_8)),
-        (9, lambda: pass_on(on_down, pass_9)),
-        (10, lambda: wait_all(pass_8, pass_9)),
+        (4, lambda: wait_all(pass_12, pass_4)),
+        (5, lambda: pass_on(own_down[1], on_down, pass_5)),
+        (5, lambda: pass_on(own_up[1], pass_13)),
+        (6, lambda: wait_all(pass_13, pass_5)),
+        (7, lambda: pass_on(on_up, pass_8)),
+        (7, lambda: pass_on(on_down, pass_9)),
+        (8, lambda: wait_all(pass_8, pass_9)),
     ]
     after = [
-        (11, lambda: finish_neighbour(0)),
-        (13, lambda: combine(0)),
-        (13, lambda: gather_own(0)),
+        (9, lambda: finish_neighbour(0)),
+        (11, lambda: combine(0)),
+        (11, lambda: gather_own(0)),
+        (12, lambda: gather_x(0)),
+        (13, lambda: gather_y(0, 0)),
+        (14, lambda: gather_y(0, 1)),
         (15, lambda: finish_neighbour(1)),
-        (15, lambda: gather_x(0)),
+        (15, lambda: gather_y2(0, 0)),
     ]
 
     def run(events, u):
@@ -404,27 +405,24 @@
     fade1[...] = jnp.ones_like(fade1)
     score(0, s0)
     lax.fori_loop(0, 16, unit, 0)
-    gather_y(0, 0)
     add_values(31, p1[...], fade1[...])
-    gather_y(0, 1)
-    combine(1)
-    gather_own(1)
-    gather_y2(0, 0)
     gather_y2(0, 1)
-    gather_x(1)
     w_copy.wait()
     gather_end(0)
     project(0)
+    combine(1)
+    gather_own(1)
+    gather_x(1)
+    reduce_added(0)
     gather_y(1, 0)
     gather_y(1, 1)
-    reduce_added(0)
     gather_y2(1, 0)
+    reduce_last(0)
     gather_y2(1, 1)
     gather_end(1)
     project(1)
-    reduce_last(0)
+    reduce_end(0)
     reduce_added(1)
-    reduce_end(0)
     reduce_last(1)
     reduce_end(1)
 

time: 85 us -> 90.2 us (1.061)
  Pallas kernels: 83.1 us -> 87.9 us
    pallas_call x1, Pallas kernels: 83.1 us -> 87.9 us  [body(): pl.pallas_call(kernel, out_shape=jax.ShapeDtypeStruct((2 * tokens, cols),...]
where the time goes in v5:
time: 90.2 us; the launch traced here: 89.5 us
  Pallas kernels  87.9 us (97%)
  local copies, waits for them, and re-layouts  1.67 us (2%)
    pallas_call x1, Pallas kernels, body(): pl.pallas_call(kernel, out_shape=jax.ShapeDtypeStruct((2 * tokens, cols),...  87.9 us

profile of v5, /device:TPU:0, one launch (start us, length us, event | category | flops | bytes accessed | tf_op | source)
XLA Modules:
  0.0 89.5 jit_solution(4706129348624144339)
XLA Ops:
  0.0 87.9 %shard_map.46 = bf16[128,1024]{1,0:T(8,128)(2,1)} custom-call(bf16[64,2048]{1,0:T(8,128)(2,1)} %q_hbm.1, bf16[1024,128]{1,0:T(8,128)(2,1)} %k_hbm.1, bf16[1024,128]{1,0:T(8,128)(2,1)} %v_hbm.1, bf16[2048,1024]{1,0:T(8,128)(2,1)} %w_hbm.1), custom_call_target="tpu_custom_call" | custom-call | flops 12999999488 | bytes 5000000 | tf_op jit(solution)/shard_map/pallas_call | solution.py:443
  87.9 1.7 %copy.6 = bf16[128,1024]{1,0:T(8,128)(2,1)} copy(bf16[128,1024]{1,0:T(8,128)(2,1)} %shard_map.46) | data formatting | bytes 524288

commit v6 on v4

--- a/solution.py
+++ b/solution.py
@@ -117,12 +117,8 @@
         mrow[r] = jnp.full((ROWS, HD), NEG, jnp.float32)
 
     def place(t):
-        v = (t - 16) % 8
-        f = (t - 16) // 8
-        pair = jnp.where(t < 8, t // 2 % 2, jnp.where(t < 16, t // 4, 4 + v // 2))
-        pair = jnp.where((t >= 16) & (v >= 4), 6 + v % 2, pair)
-        row = jnp.where(t < 8, t // 4 * 2 + t % 2, jnp.where(t < 16, t % 4, v % 2 * 2 + f))
-        row = jnp.where((t >= 16) & (v >= 4), (1 - (v - 4) // 2) * 2 + f, row)
+        pair = jnp.where(t < 8, t // 2 % 2, t // 4)
+        row = jnp.where(t < 8, t // 4 * 2 + t % 2, jnp.where(t < 24, t % 4, (t + 2) % 4))
         i = pair - 2
         middle = 12 + 2 * (i % 2) + i // 2
         one = jnp.where(pair < 2, 2 * pair, jnp.where(pair < 6, middle, 2 * pair - 4))
@@ -364,17 +360,14 @@
         (5, lambda: wait_all(pass_12, pass_4)),
         (7, lambda: pass_on(own_down[1], on_down, pass_5)),
         (7, lambda: pass_on(own_up[1], pass_13)),
-        (8, lambda: wait_all(pass_13, pass_5)),
-        (9, lambda: pass_on(on_up, pass_8)),
-        (9, lambda: pass_on(on_down, pass_9)),
-        (10, lambda: wait_all(pass_8, pass_9)),
+        (9, lambda: wait_all(pass_13, pass_5)),
+        (11, lambda: pass_on(on_up, pass_8)),
+        (11, lambda: pass_on(on_down, pass_9)),
+        (13, lambda: wait_all(pass_8, pass_9)),
     ]
     after = [
-        (11, lambda: finish_neighbour(0)),
-        (13, lambda: combine(0)),
-        (13, lambda: gather_own(0)),
+        (14, lambda: finish_neighbour(0)),
         (15, lambda: finish_neighbour(1)),
-        (15, lambda: gather_x(0)),
     ]
 
     def run(events, u):
@@ -404,21 +397,24 @@
     fade1[...] = jnp.ones_like(fade1)
     score(0, s0)
     lax.fori_loop(0, 16, unit, 0)
+    combine(0)
+    gather_own(0)
+    add_values(31, p1[...], fade1[...])
+    combine(1)
+    gather_x(0)
     gather_y(0, 0)
-    add_values(31, p1[...], fade1[...])
+    gather_own(1)
     gather_y(0, 1)
-    combine(1)
-    gather_own(1)
+    gather_x(1)
     gather_y2(0, 0)
+    gather_y(1, 0)
     gather_y2(0, 1)
-    gather_x(1)
     w_copy.wait()
     gather_end(0)
     project(0)
-    gather_y(1, 0)
     gather_y(1, 1)
+    gather_y2(1, 0)
     reduce_added(0)
-    gather_y2(1, 0)
     gather_y2(1, 1)
     gather_end(1)
     project(1)

time: 85 us -> 88.4 us (1.040)
  Pallas kernels: 83.1 us -> 86.6 us
    pallas_call x1, Pallas kernels: 83.1 us -> 86.6 us  [body(): pl.pallas_call(kernel, out_shape=jax.ShapeDtypeStruct((2 * tokens, cols),...]
where the time goes in v6:
time: 88.4 us; the launch traced here: 88.3 us
  Pallas kernels  86.6 us (98%)
  local copies, waits for them, and re-layouts  1.67 us (2%)
    pallas_call x1, Pallas kernels, body(): pl.pallas_call(kernel, out_shape=jax.ShapeDtypeStruct((2 * tokens, cols),...  86.6 us

profile of v6, /device:TPU:0, one launch (start us, length us, event | category | flops | bytes accessed | tf_op | source)
XLA Modules:
  0.0 88.3 jit_solution(8846619361606450897)
XLA Ops:
  0.0 86.6 %shard_map.46 = bf16[128,1024]{1,0:T(8,128)(2,1)} custom-call(bf16[64,2048]{1,0:T(8,128)(2,1)} %q_hbm.1, bf16[1024,128]{1,0:T(8,128)(2,1)} %k_hbm.1, bf16[1024,128]{1,0:T(8,128)(2,1)} %v_hbm.1, bf16[2048,1024]{1,0:T(8,128)(2,1)} %w_hbm.1), custom_call_target="tpu_custom_call" | custom-call | flops 12999999488 | bytes 5000000 | tf_op jit(solution)/shard_map/pallas_call | solution.py:441
  86.6 1.7 %copy.6 = bf16[128,1024]{1,0:T(8,128)(2,1)} copy(bf16[128,1024]{1,0:T(8,128)(2,1)} %shard_map.46) | data formatting | bytes 524288

commit v7 on v4

--- a/solution.py
+++ b/solution.py
@@ -117,12 +117,13 @@
         mrow[r] = jnp.full((ROWS, HD), NEG, jnp.float32)
 
     def place(t):
-        v = (t - 16) % 8
-        f = (t - 16) // 8
-        pair = jnp.where(t < 8, t // 2 % 2, jnp.where(t < 16, t // 4, 4 + v // 2))
-        pair = jnp.where((t >= 16) & (v >= 4), 6 + v % 2, pair)
-        row = jnp.where(t < 8, t // 4 * 2 + t % 2, jnp.where(t < 16, t % 4, v % 2 * 2 + f))
-        row = jnp.where((t >= 16) & (v >= 4), (1 - (v - 4) // 2) * 2 + f, row)
+        v = t % 8
+        early = jnp.where(v < 4, 4 + v // 2, 6 + v % 2)
+        early_row = jnp.where(v < 4, v % 2, 1 - (v - 4) // 2) * 2
+        pair = jnp.where(t < 8, t // 2 % 2, jnp.where(t < 16, t // 4, early))
+        pair = jnp.where(t < 24, pair, 4 + t % 4)
+        row = jnp.where(t < 8, t // 4 * 2 + t % 2, jnp.where(t < 16, t % 4, early_row))
+        row = jnp.where(t < 24, row, (1 - v // 4) * 2 + 1)
         i = pair - 2
         middle = 12 + 2 * (i % 2) + i // 2
         one = jnp.where(pair < 2, 2 * pair, jnp.where(pair < 6, middle, 2 * pair - 4))
@@ -294,14 +295,15 @@
     ]
     side_copy = [remote(side.at[f], side_in.at[f], S_SIDE + f, to_side) for f in range(2)]
 
-    def project(f):
-        for i in range(2):
-            terms[f, :, half(i)] = jnp.dot(
-                att[f], w[:, half(i)], preferred_element_type=jnp.float32
-            ).astype(jnp.bfloat16)
+    def project(f, part):
+        lanes = slice(part * (cols // 2), (part + 1) * (cols // 2))
+        terms[f, :, lanes] = jnp.dot(
+            att[f], w[:, lanes], preferred_element_type=jnp.float32
+        ).astype(jnp.bfloat16)
+        if part % 2 == 1:
+            i = part // 2
             far_copy[f][i].start()
-        for i in range(2):
-            plain_copy[f][i].start()
+            plain_copy[f][1 - i].start()
 
     def reduce_added(f):
         for i in range(2):
@@ -373,7 +375,7 @@
         (11, lambda: finish_neighbour(0)),
         (13, lambda: combine(0)),
         (13, lambda: gather_own(0)),
-        (15, lambda: finish_neighbour(1)),
+        (14, lambda: finish_neighbour(1)),
         (15, lambda: gather_x(0)),
     ]
 
@@ -404,24 +406,30 @@
     fade1[...] = jnp.ones_like(fade1)
     score(0, s0)
     lax.fori_loop(0, 16, unit, 0)
-    gather_y(0, 0)
     add_values(31, p1[...], fade1[...])
-    gather_y(0, 1)
     combine(1)
     gather_own(1)
+    gather_y(0, 0)
+    gather_y(0, 1)
+    gather_x(1)
     gather_y2(0, 0)
+    gather_y(1, 0)
     gather_y2(0, 1)
-    gather_x(1)
     w_copy.wait()
     gather_end(0)
-    project(0)
-    gather_y(1, 0)
+    project(0, 0)
     gather_y(1, 1)
+    project(0, 1)
+    gather_y2(1, 0)
+    project(0, 2)
+    gather_y2(1, 1)
+    project(0, 3)
+    gather_end(1)
+    project(1, 0)
+    project(1, 1)
     reduce_added(0)
-    gather_y2(1, 0)
-    gather_y2(1, 1)
-    gather_end(1)
-    project(1)
+    project(1, 2)
+    project(1, 3)
     reduce_last(0)
     reduce_added(1)
     reduce_end(0)

time: 85 us -> 88.5 us (1.041)
  Pallas kernels: 83.1 us -> 86.7 us
    pallas_call x1, Pallas kernels: 83.1 us -> 86.7 us  [body(): pl.pallas_call(kernel, out_shape=jax.ShapeDtypeStruct((2 * tokens, cols),...]
where the time goes in v7:
time: 88.5 us; the launch traced here: 88.4 us
  Pallas kernels  86.7 us (98%)
  local copies, waits for them, and re-layouts  1.67 us (2%)
    pallas_call x1, Pallas kernels, body(): pl.pallas_call(kernel, out_shape=jax.ShapeDtypeStruct((2 * tokens, cols),...  86.7 us

profile of v7, /device:TPU:0, one launch (start us, length us, event | category | flops | bytes accessed | tf_op | source)
XLA Modules:
  0.0 88.4 jit_solution(11252907378093362041)
XLA Ops:
  0.0 86.7 %shard_map.46 = bf16[128,1024]{1,0:T(8,128)(2,1)} custom-call(bf16[64,2048]{1,0:T(8,128)(2,1)} %q_hbm.1, bf16[1024,128]{1,0:T(8,128)(2,1)} %k_hbm.1, bf16[1024,128]{1,0:T(8,128)(2,1)} %v_hbm.1, bf16[2048,1024]{1,0:T(8,128)(2,1)} %w_hbm.1), custom_call_target="tpu_custom_call" | custom-call | flops 12999999488 | bytes 5000000 | tf_op jit(solution)/shard_map/pallas_call | solution.py:453
  86.7 1.7 %copy.6 = bf16[128,1024]{1,0:T(8,128)(2,1)} copy(bf16[128,1024]{1,0:T(8,128)(2,1)} %shard_map.46) | data formatting | bytes 524288

commit v8 on v7

--- a/solution.py
+++ b/solution.py
@@ -21,34 +21,27 @@
 S_O = 16
 S_STAT = 18
 S_ATT = 20
-S_FAR = 54
-S_PLAIN = 58
-S_LATER = 62
-S_SIDE = 66
-S_COUNT = 68
+S_COUNT = 54
 
 
 def device_at(x, y, core):
     return x * 8 + y * 2 + core
 
 
-def kernel(
-    q_hbm, k_hbm, v_hbm, w_hbm, out_ref,
+def attend_kernel(
+    q_hbm, k_hbm, v_hbm, att,
     q_ref, k_ref, q_s, kv, s0, s1, p1, fade1, acc, mrow, o_send, s_send, o_recv, s_recv,
-    att, w, terms, far_in, plain_in, added, added_in, side, side_in, mine, fetched, send, recv,
+    own, fetched, send, recv,
 ):
     c, h = lax.axis_index("ctx"), lax.axis_index("head")
     x, y, core = c // 8, (c // 2) % 4, c % 2
-    z, e = h // 2, h % 2
     scale = LOG2E / math.sqrt(HD)
 
     to_core = (device_at(x, y, 1 - core), h)
     to_up = (device_at(x, (y + 1) % 4, core), h)
     to_down = (device_at(x, (y + 3) % 4, core), h)
     to_x = (device_at(1 - x, y, core), h)
-    z_ways = ((c, ((z + 1) % 4) * 2 + e), (c, ((z + 3) % 4) * 2 + e))
-    to_side = (c, z * 2 + 1 - e)
-    partners = (to_core, to_up, to_down, to_x, to_side) + z_ways
+    partners = (to_core, to_up, to_down, to_x)
 
     def remote(src, dst, number, where):
         return pltpu.make_async_remote_copy(
@@ -64,7 +57,6 @@
         )
         for i in range(2)
     ]
-    w_copy = pltpu.make_async_copy(w_hbm, w, fetched.at[4])
     for fetch in [k_fetch, q_fetch] + v_fetch:
         fetch.start()
     barrier = pltpu.get_barrier_semaphore()
@@ -85,7 +77,6 @@
             ]
     for fetch in v_fetch:
         fetch.wait()
-    w_copy.start()
     pl.semaphore_wait(barrier, len(partners))
 
     def kv_copy(number, source, target, where):
@@ -188,6 +179,11 @@
         start = owner * HALF
         return start if isinstance(start, int) else pl.multiple_of(start, HALF)
 
+    keep = [
+        pltpu.make_async_copy(own.at[f], att.at[f, pl.ds(block_of(c), HALF)], fetched.at[4 + f])
+        for f in range(2)
+    ]
+
     def combine(f):
         value, level = normalised(f)
         o_copy[f].wait_recv()
@@ -198,9 +194,8 @@
         done = (value * part_a + o_recv[f].astype(jnp.float32) * part_b) / (part_a + part_b)
         done = done.astype(jnp.bfloat16)
         for i in range(16):
-            att[f, pl.ds(block_of(c), HALF), i * HD : (i + 1) * HD] = done[
-                i * HALF : (i + 1) * HALF
-            ]
+            own[f, :, i * HD : (i + 1) * HD] = done[i * HALF : (i + 1) * HALF]
+        keep[f].start()
 
     def gather_copy(f, number, dx, dy, where, part=None, from_core=None):
         owner = device_at(1 - x if dx else x, (y + dy) % 4, core if from_core is None else from_core)
@@ -209,7 +204,8 @@
             size = HALF // 2
             start = pl.multiple_of(start + part * size, size)
         block = att.at[f, pl.ds(start, size)]
-        return remote(block, block, S_ATT + 17 * f + number, where)
+        mine = dx == 0 and dy == 0 and from_core is None
+        return remote(own.at[f] if mine else block, block, S_ATT + 17 * f + number, where)
 
     sent = own_up + own_down + own_core + [pass_12, pass_4, pass_13, pass_5, on_up, on_down]
     sent += [pass_8, pass_9] + q_copy + o_copy + s_copy
@@ -259,89 +255,6 @@
             copies += [gather_copy(f, 13 + plane, plane, 3, to_up, 0)]
             copies += [gather_copy(f, 15 + plane, plane, 1, to_down, 1)]
         return copies
-
-    cols = w.shape[1] // 2
-    rows = 4 * HALF
-
-    def half(i):
-        return pl.ds(i * cols, cols)
-
-    def block(distance):
-        return pl.ds(pl.multiple_of(((z + distance) % 4) * rows, rows), rows)
-
-    far_copy = [
-        [
-            remote(terms.at[f, block(2), half(i)], far_in.at[f, i], S_FAR + 2 * f + i, z_ways[i])
-            for i in range(2)
-        ]
-        for f in range(2)
-    ]
-    plain_copy = [
-        [
-            remote(
-                terms.at[f, block(1 + 2 * i), half(1 - i)], plain_in.at[f, i],
-                S_PLAIN + 2 * f + i, z_ways[i],
-            )
-            for i in range(2)
-        ]
-        for f in range(2)
-    ]
-    later_copy = [
-        [
-            remote(added.at[f, i], added_in.at[f, i], S_LATER + 2 * f + i, z_ways[i])
-            for i in range(2)
-        ]
-        for f in range(2)
-    ]
-    side_copy = [remote(side.at[f], side_in.at[f], S_SIDE + f, to_side) for f in range(2)]
-
-    def project(f, part):
-        lanes = slice(part * (cols // 2), (part + 1) * (cols // 2))
-        terms[f, :, lanes] = jnp.dot(
-            att[f], w[:, lanes], preferred_element_type=jnp.float32
-        ).astype(jnp.bfloat16)
-        if part % 2 == 1:
-            i = part // 2
-            far_copy[f][i].start()
-            plain_copy[f][1 - i].start()
-
-    def reduce_added(f):
-        for i in range(2):
-            far_copy[f][i].wait_recv()
-            added[f, i] = (
-                terms[f, block(1 + 2 * i), half(i)].astype(jnp.float32)
-                + far_in[f, i].astype(jnp.float32)
-            ).astype(jnp.bfloat16)
-            later_copy[f][i].start()
-
-    def reduce_last(f):
-        for i in range(2):
-            plain_copy[f][i].wait_recv()
-        for i in range(2):
-            later_copy[f][i].wait_recv()
-
-        def summed(s, i):
-            size = rows // 2
-            part = pl.ds(pl.multiple_of(s * size, size), size)
-            own = pl.ds(pl.multiple_of(z * rows + s * size, size), size)
-            return (
-                terms[f, own, half(i)].astype(jnp.float32)
-                + added_in[f, i, part].astype(jnp.float32)
-                + plain_in[f, 1 - i, part].astype(jnp.float32)
-            )
-
-        for i in range(2):
-            side[f, :, half(i)] = summed(1 - e, i).astype(jnp.bfloat16)
-        side_copy[f].start()
-        for i in range(2):
-            mine[f, :, half(i)] = summed(e, i)
-
-    def reduce_end(f):
-        side_copy[f].wait_recv()
-        done = (mine[f] + side_in[f].astype(jnp.float32)).astype(jnp.bfloat16)
-        for i in range(2):
-            start = i * RUN + f * HALF
-            out_ref[start : start + HALF] = done[i * HALF : (i + 1) * HALF]
 
     def wait_all(*copies):
         for copy in copies:
@@ -415,32 +328,120 @@
     gather_y2(0, 0)
     gather_y(1, 0)
     gather_y2(0, 1)
-    w_copy.wait()
+    gather_y(1, 1)
+    gather_y2(1, 0)
+    gather_y2(1, 1)
     gather_end(0)
-    project(0, 0)
-    gather_y(1, 1)
-    project(0, 1)
-    gather_y2(1, 0)
-    project(0, 2)
-    gather_y2(1, 1)
-    project(0, 3)
     gather_end(1)
-    project(1, 0)
-    project(1, 1)
-    reduce_added(0)
-    project(1, 2)
-    project(1, 3)
-    reduce_last(0)
-    reduce_added(1)
-    reduce_end(0)
-    reduce_last(1)
-    reduce_end(1)
-
-    sent += side_copy
+
     for f in range(2):
-        sent += gather_sent(f) + far_copy[f] + plain_copy[f] + later_copy[f]
+        keep[f].wait()
+        sent += gather_sent(f)
     for copy in sent:
         copy.wait_send()
+
+
+def reduce_kernel(terms, out_ref, far_in, plain_in, added, added_in, side, side_in, send, recv):
+    c, h = lax.axis_index("ctx"), lax.axis_index("head")
+    z, e = h // 2, h % 2
+    cols = out_ref.shape[1] // 2
+    size = 2 * HALF
+    ways = ((c, ((z + 1) % 4) * 2 + e), (c, ((z + 3) % 4) * 2 + e))
+    to_side = (c, z * 2 + 1 - e)
+
+    barrier = pltpu.get_barrier_semaphore()
+    for partner in ways + (to_side,):
+        pl.semaphore_signal(barrier, inc=1, device_id=partner, device_id_type=MESH)
+    pl.semaphore_wait(barrier, 3)
+
+    def copy_of(number, source, target, where):
+        return pltpu.make_async_remote_copy(
+            src_ref=source, dst_ref=target, send_sem=send.at[number], recv_sem=recv.at[number],
+            device_id=where, device_id_type=MESH,
+        )
+
+    def half(i):
+        return pl.ds(i * cols, cols)
+
+    def block(distance, g):
+        side_of = e if g == 1 else 1 - e
+        return pl.ds(pl.multiple_of((((z + distance) % 4) * 2 + side_of) * size, size), size)
+
+    both = pl.ds(0, 2)
+    far = [
+        [
+            copy_of(2 * g + i, terms.at[both, block(2, g), half(i)], far_in.at[g, i], ways[i])
+            for i in range(2)
+        ]
+        for g in range(2)
+    ]
+    plain = [
+        [
+            copy_of(
+                4 + 2 * g + i, terms.at[both, block(1 + 2 * i, g), half(1 - i)],
+                plain_in.at[g, i], ways[i],
+            )
+            for i in range(2)
+        ]
+        for g in range(2)
+    ]
+    later = [
+        [copy_of(8 + 2 * g + i, added.at[g, i], added_in.at[g, i], ways[i]) for i in range(2)]
+        for g in range(2)
+    ]
+    across = copy_of(12, side, side_in, to_side)
+
+    def add_on(g):
+        for i in range(2):
+            far[g][i].wait_recv()
+            added[g, i] = (
+                terms[:, block(1 + 2 * i, g), half(i)].astype(jnp.float32)
+                + far_in[g, i].astype(jnp.float32)
+            ).astype(jnp.bfloat16)
+            later[g][i].start()
+
+    def summed(g, i):
+        return (
+            terms[:, block(0, g), half(i)].astype(jnp.float32)
+            + added_in[g, i].astype(jnp.float32)
+            + plain_in[g, 1 - i].astype(jnp.float32)
+        )
+
+    def wait_sums(g):
+        for i in range(2):
+            plain[g][i].wait_recv()
+        for i in range(2):
+            later[g][i].wait_recv()
+
+    for copies in far + plain[:1]:
+        for copy in copies:
+            copy.start()
+    add_on(0)
+    for copy in plain[1]:
+        copy.start()
+    add_on(1)
+    wait_sums(0)
+    for i in range(2):
+        side[:, :, half(i)] = summed(0, i).astype(jnp.bfloat16)
+    across.start()
+    wait_sums(1)
+    across.wait_recv()
+    for i in range(2):
+        done = (summed(1, i) + side_in[:, :, half(i)].astype(jnp.float32)).astype(jnp.bfloat16)
+        for f in range(2):
+            for k in range(2):
+                start = k * RUN + f * HALF
+                out_ref[start : start + HALF, half(i)] = done[f, k * HALF : (k + 1) * HALF]
+    for copies in far + plain + later:
+        for copy in copies:
+            copy.wait_send()
+    across.wait_send()
+
+
+def params(number, mib):
+    return pltpu.CompilerParams(
+        collective_id=number, has_side_effects=True, vmem_limit_bytes=mib * 1024 * 1024
+    )
 
 
 def body(queries, key_cache, value_cache, out_weight):
@@ -449,12 +450,11 @@
     all_rows = tokens // 2 * lax.axis_size("ctx")
     vmem, anywhere = pl.BlockSpec(memory_space=pltpu.VMEM), pl.BlockSpec(memory_space=pl.ANY)
     bf16, f32 = jnp.bfloat16, jnp.float32
-    piece = pltpu.VMEM((2, 2, 2 * tokens, cols // 2), bf16)
-    return pl.pallas_call(
-        kernel,
-        out_shape=jax.ShapeDtypeStruct((2 * tokens, cols), bf16),
-        in_specs=[anywhere] * 4,
-        out_specs=vmem,
+    attended = pl.pallas_call(
+        attend_kernel,
+        out_shape=jax.ShapeDtypeStruct((2, all_rows, width), bf16),
+        in_specs=[anywhere] * 3,
+        out_specs=anywhere,
         scratch_shapes=[
             pltpu.VMEM(queries.shape, bf16),
             pltpu.VMEM(key_cache.shape, bf16),
@@ -470,27 +470,37 @@
             pltpu.VMEM((2, 8, ROWS), f32),
             pltpu.VMEM((2, ROWS, HD), bf16),
             pltpu.VMEM((2, 8, ROWS), f32),
-            pltpu.VMEM((2, all_rows, width), bf16),
-            pltpu.VMEM(out_weight.shape, bf16),
-            pltpu.VMEM((2, all_rows, cols), bf16),
+            pltpu.VMEM((2, tokens // 2, width), bf16),
+            pltpu.SemaphoreType.DMA((6,)),
+            pltpu.SemaphoreType.DMA((S_COUNT,)),
+            pltpu.SemaphoreType.DMA((S_COUNT,)),
+        ],
+        compiler_params=params(0, 58),
+        cost_estimate=pl.CostEstimate(
+            flops=8_600_000_000, bytes_accessed=5_000_000, transcendentals=17_000_000
+        ),
+    )(queries, key_cache, value_cache)
+    terms = jnp.dot(
+        attended.reshape(2 * all_rows, width), out_weight, preferred_element_type=f32
+    ).astype(bf16)
+    piece = pltpu.VMEM((2, 2, 2, tokens, cols // 2), bf16)
+    return pl.pallas_call(
+        reduce_kernel,
+        out_shape=jax.ShapeDtypeStruct((2 * tokens, cols), bf16),
+        in_specs=[vmem],
+        out_specs=vmem,
+        scratch_shapes=[
             piece,
             piece,
             piece,
             piece,
             pltpu.VMEM((2, tokens, cols), bf16),
             pltpu.VMEM((2, tokens, cols), bf16),
-            pltpu.VMEM((2, tokens, cols), f32),
-            pltpu.SemaphoreType.DMA((5,)),
-            pltpu.SemaphoreType.DMA((S_COUNT,)),
-            pltpu.SemaphoreType.DMA((S_COUNT,)),
+            pltpu.SemaphoreType.DMA((13,)),
+            pltpu.SemaphoreType.DMA((13,)),
         ],
-        compiler_params=pltpu.CompilerParams(
-            collective_id=0, has_side_effects=True, vmem_limit_bytes=56 * 1024 * 1024
-        ),
-        cost_estimate=pl.CostEstimate(
-            flops=13_000_000_000, bytes_accessed=5_000_000, transcendentals=17_000_000
-        ),
-    )(queries, key_cache, value_cache, out_weight)
+        compiler_params=params(1, 16),
+    )(terms.reshape(2, all_rows, cols))
 
 
 def solution(mesh):

time: 88.5 us -> 96 us (1.085)
  matrix products: 0 us -> 6.9 us
  Pallas kernels: 86.7 us -> 88.2 us
  local copies, waits for them, and re-layouts: 1.67 us -> 0.71 us
    dot_general x0 -> x1, matrix products: none -> 6.9 us  [body(): jnp.dot(attended.reshape(2 * all_rows, width), out_weight, preferred_elem...]
    pallas_call x1 -> x2, Pallas kernels: 86.7 us -> 88.2 us  [the longest x1 61.7 us: body(): pl.pallas_call(attend_kernel, out_shape=jax.ShapeDtypeStruct((2, all_rows...]
    unnamed x1 -> x3, local copies, waits for them, and re-layouts: 1.67 us -> 0.71 us
where the time goes in v8:
time: 96 us; the launch traced here: 95.9 us
  Pallas kernels  88.2 us (92%)
  matrix products  6.9 us (7%)
    pallas_call x1, Pallas kernels, body(): pl.pallas_call(attend_kernel, out_shape=jax.ShapeDtypeStruct((2, all_rows...  61.7 us
    pallas_call x1, Pallas kernels, body(): pl.pallas_call(reduce_kernel, out_shape=jax.ShapeDtypeStruct((2 * tokens,...  26.5 us
    dot_general x1, matrix products, body(): jnp.dot(attended.reshape(2 * all_rows, width), out_weight, preferred_elem...  6.9 us

profile of v8, /device:TPU:0, one launch (start us, length us, event | category | flops | bytes accessed | tf_op | source)
XLA Modules:
  0.0 95.9 jit_solution(14335906647873546034)
XLA Ops:
  0.0 0.0 copy-start
  0.0 61.7 %shard_map.46 = bf16[2,512,2048]{2,1,0:T(8,128)(2,1)} custom-call(bf16[64,2048]{1,0:T(8,128)(2,1)} %q_hbm.1, bf16[1024,128]{1,0:T(8,128)(2,1)} %k_hbm.1, bf16[1024,128]{1,0:T(8,128)(2,1)} %v_hbm.1), custom_call_target="tpu_custom_call" | custom-call | flops 8600000512 | bytes 5000000 | tf_op jit(solution)/shard_map/pallas_call | solution.py:453
  61.7 0.0 copy-done
  61.7 6.9 %convolution_convert_fusion = bf16[1024,1024]{1,0:T(8,128)(2,1)S(1)} fusion(bf16[1024,2048]{1,0:T(8,128)(2,1)} %bitcast.5, bf16[2048,1024]{1,0:T(8,128)(2,1)S(1)} %copy-done), kind=kOutput, calls=%fused_computation | convolution fusion | flops 4296015872 | bytes 10485760 | tf_op jit(solution)/shard_map/dot_general | solution.py:483
  68.6 26.5 %shard_map.47 = bf16[128,1024]{1,0:T(8,128)(2,1)S(1)} custom-call(bf16[2,512,1024]{2,1,0:T(8,128)(2,1)S(1)} %bitcast.4), custom_call_target="tpu_custom_call" | custom-call | tf_op jit(solution)/shard_map/pallas_call | solution.py:487
  95.2 0.7 copy.6
Async XLA Ops:
  0.0 61.7 %copy-start = (bf16[2048,1024]{1,0:T(8,128)(2,1)S(1)}, bf16[2048,1024]{1,0:T(8,128)(2,1)}, u32[]{:S(2)}) copy-start(bf16[2048,1024]{1,0:T(8,128)(2,1)} %param.7) | copy-start | bytes 12582916

commit v9 on v6

--- a/solution.py
+++ b/solution.py
@@ -34,7 +34,7 @@
 
 def kernel(
     q_hbm, k_hbm, v_hbm, w_hbm, out_ref,
-    q_ref, k_ref, q_s, kv, s0, s1, p1, fade1, acc, mrow, o_send, s_send, o_recv, s_recv,
+    q_ref, k_ref, q_s, kv, keys, values, s0, s1, p1, fade1, acc, mrow, o_send, s_send, o_recv, s_recv,
     att, w, terms, far_in, plain_in, added, added_in, side, side_in, mine, fetched, send, recv,
 ):
     c, h = lax.axis_index("ctx"), lax.axis_index("head")
@@ -116,33 +116,31 @@
         acc[r] = jnp.zeros((ROWS, 2 * HD), jnp.float32)
         mrow[r] = jnp.full((ROWS, HD), NEG, jnp.float32)
 
-    def place(t):
-        pair = jnp.where(t < 8, t // 2 % 2, t // 4)
-        row = jnp.where(t < 8, t // 4 * 2 + t % 2, jnp.where(t < 24, t % 4, (t + 2) % 4))
+    def slots_of(pair):
         i = pair - 2
         middle = 12 + 2 * (i % 2) + i // 2
         one = jnp.where(pair < 2, 2 * pair, jnp.where(pair < 6, middle, 2 * pair - 4))
         two = jnp.where((pair >= 2) & (pair < 6), one - 8, one + 1)
-        return one, two, row
-
-    def score(t, s_ref):
-        one, two, row = place(t)
-        queries = q_s[row]
-        for j, slot in enumerate((one, two)):
-            keys = jnp.concatenate(
-                [kv[slot, KEYS + b * HD : KEYS + (b + 1) * HD] for b in range(4)], axis=1
-            )
-            s_ref[:, j * KEYS : (j + 1) * KEYS] = (
-                jnp.dot(queries, keys, preferred_element_type=jnp.float32) * scale
-            )
-
-    def weigh(t, s_ref):
-        one, two, row = place(t)
-        asker = device_at(jnp.where(row >= 2, 1 - x, x), y, core)
+        return one, two
+
+    def stage(pair, where):
+        for j, slot in enumerate(slots_of(pair)):
+            for b in range(4):
+                start = j * KEYS + b * HD
+                keys[where, :, start : start + HD] = kv[slot, KEYS + b * HD : KEYS + (b + 1) * HD]
+            values[where, j * KEYS : (j + 1) * KEYS, 0:HD] = kv[slot, 0:KEYS]
+
+    def score(row, where, s_ref):
+        s_ref[...] = (
+            jnp.dot(q_s[row], keys[where], preferred_element_type=jnp.float32) * scale
+        )
+
+    def weigh(pair, row, s_ref):
+        asker = device_at(1 - x if row >= 2 else x, y, core)
         token = lax.broadcasted_iota(jnp.int32, (ROWS, HD), 0) % HALF
         key_token = lax.broadcasted_iota(jnp.int32, (ROWS, HD), 1) - RUN
         pieces = []
-        for j, slot in enumerate((one, two)):
+        for j, slot in enumerate(slots_of(pair)):
             holder_core = jnp.where((slot // 2) % 2 == 1, 1 - core, core)
             holder = device_at(x, (y + slot // 4) % 4, holder_core)
             first = jnp.where(slot % 2 == 1, holder * RUN, -(1 << 20))
@@ -158,14 +156,9 @@
         mrow[row] = new
         return weights.astype(jnp.bfloat16), jnp.exp2(old - new)
 
-    def add_values(t, weights, fade):
-        one, two, row = place(t)
-        ones = jnp.ones((KEYS, HD), jnp.bfloat16)
-        values = jnp.concatenate(
-            [jnp.concatenate([kv[slot, 0:KEYS], ones], axis=1) for slot in (one, two)], axis=0
-        )
+    def add_values(row, where, weights, fade):
         acc[row] = acc[row] * jnp.concatenate([fade, fade], axis=1) + jnp.dot(
-            weights, values, preferred_element_type=jnp.float32
+            weights, values[where], preferred_element_type=jnp.float32
         )
 
     def normalised(row):
@@ -351,23 +344,18 @@
         own_up[1].start()
         own_down[1].start()
 
-    before = [
+    amid = [
         (0, start_rest),
-        (1, lambda: wait_all(q_copy[0])),
-        (2, lambda: wait_all(q_copy[1])),
-        (3, lambda: pass_on(own_up[0], on_up, pass_12)),
-        (3, lambda: pass_on(own_down[0], pass_4)),
-        (5, lambda: wait_all(pass_12, pass_4)),
-        (7, lambda: pass_on(own_down[1], on_down, pass_5)),
-        (7, lambda: pass_on(own_up[1], pass_13)),
-        (9, lambda: wait_all(pass_13, pass_5)),
-        (11, lambda: pass_on(on_up, pass_8)),
-        (11, lambda: pass_on(on_down, pass_9)),
-        (13, lambda: wait_all(pass_8, pass_9)),
-    ]
-    after = [
-        (14, lambda: finish_neighbour(0)),
-        (15, lambda: finish_neighbour(1)),
+        (1, lambda: pass_on(own_up[0], on_up, pass_12)),
+        (1, lambda: pass_on(own_down[0], pass_4)),
+        (2, lambda: wait_all(pass_12, pass_4)),
+        (3, lambda: pass_on(own_down[1], on_down, pass_5)),
+        (3, lambda: pass_on(own_up[1], pass_13)),
+        (4, lambda: wait_all(pass_13, pass_5)),
+        (5, lambda: pass_on(on_up, pass_8)),
+        (5, lambda: pass_on(on_down, pass_9)),
+        (6, lambda: wait_all(pass_8, pass_9)),
+        (7, lambda: finish_neighbour(0)),
     ]
 
     def run(events, u):
@@ -379,27 +367,40 @@
                     if step == k:
                         action()
 
-    def unit(u, carry):
-        run(before, u)
-        t = 2 * u
-        score(t + 1, s1)
-        weights, fade = weigh(t, s0)
-        add_values(jnp.maximum(t - 1, 0), p1[...], fade1[...])
-        score(jnp.minimum(t + 2, 31), s0)
-        weights_1, fade_1 = weigh(t + 1, s1)
-        add_values(t, weights, fade)
-        p1[...] = weights_1
-        fade1[...] = fade_1
-        run(after, u)
+    def two_pairs(step, carry):
+        for now in range(2):
+            pair, then = 2 * step + now, 1 - now
+            score(3, now, s1)
+            weights_a, fade_a = weigh(pair, 2, s0)
+            add_values(1, then, p1[...], fade1[...])
+            score(0, now, s0)
+            weights_b, fade_b = weigh(pair, 3, s1)
+            add_values(2, now, weights_a, fade_a)
+            run([(k, action) for k, action in amid if k % 2 == now], pair)
+            stage(jnp.minimum(pair + 1, 7), then)
+            score(1, now, s1)
+            weights_c, fade_c = weigh(pair, 0, s0)
+            add_values(3, now, weights_b, fade_b)
+            score(2, then, s0)
+            weights_d, fade_d = weigh(pair, 1, s1)
+            add_values(0, now, weights_c, fade_c)
+            p1[...] = weights_d
+            fade1[...] = fade_d
         return carry
 
     p1[...] = jnp.zeros_like(p1)
     fade1[...] = jnp.ones_like(fade1)
-    score(0, s0)
-    lax.fori_loop(0, 16, unit, 0)
+    for i in range(2):
+        values[i, :, 0:HD] = jnp.zeros((2 * KEYS, HD), jnp.bfloat16)
+        values[i, :, HD : 2 * HD] = jnp.ones((2 * KEYS, HD), jnp.bfloat16)
+    stage(0, 0)
+    wait_all(*q_copy)
+    score(2, 0, s0)
+    lax.fori_loop(0, 4, two_pairs, 0)
+    finish_neighbour(1)
+    add_values(1, 1, p1[...], fade1[...])
     combine(0)
     gather_own(0)
-    add_values(31, p1[...], fade1[...])
     combine(1)
     gather_x(0)
     gather_y(0, 0)
@@ -448,6 +449,8 @@
             pltpu.VMEM(key_cache.shape, bf16),
             pltpu.VMEM((4, ROWS, HD), bf16),
             pltpu.VMEM((16, 2 * KEYS, HD), bf16),
+            pltpu.VMEM((2, HD, 2 * KEYS), bf16),
+            pltpu.VMEM((2, 2 * KEYS, 2 * HD), bf16),
             pltpu.VMEM((ROWS, 2 * KEYS), f32),
             pltpu.VMEM((ROWS, 2 * KEYS), f32),
             pltpu.VMEM((ROWS, 2 * KEYS), bf16),

time: 88.4 us -> 89.8 us (1.016)
  Pallas kernels: 86.6 us -> 88 us
    pallas_call x1, Pallas kernels: 86.6 us -> 88 us  [body(): pl.pallas_call(kernel, out_shape=jax.ShapeDtypeStruct((2 * tokens, cols),...]
where the time goes in v9:
time: 89.8 us; the launch traced here: 89.7 us
  Pallas kernels  88 us (98%)
  local copies, waits for them, and re-layouts  1.67 us (2%)
    pallas_call x1, Pallas kernels, body(): pl.pallas_call(kernel, out_shape=jax.ShapeDtypeStruct((2 * tokens, cols),...  88 us

profile of v9, /device:TPU:0, one launch (start us, length us, event | category | flops | bytes accessed | tf_op | source)
XLA Modules:
  0.0 89.7 jit_solution(8422272658945261335)
XLA Ops:
  0.0 88.0 %shard_map.46 = bf16[128,1024]{1,0:T(8,128)(2,1)} custom-call(bf16[64,2048]{1,0:T(8,128)(2,1)} %q_hbm.1, bf16[1024,128]{1,0:T(8,128)(2,1)} %k_hbm.1, bf16[1024,128]{1,0:T(8,128)(2,1)} %v_hbm.1, bf16[2048,1024]{1,0:T(8,128)(2,1)} %w_hbm.1), custom_call_target="tpu_custom_call" | custom-call | flops 12999999488 | bytes 5000000 | tf_op jit(solution)/shard_map/pallas_call | solution.py:442
  88.0 1.7 %copy.6 = bf16[128,1024]{1,0:T(8,128)(2,1)} copy(bf16[128,1024]{1,0:T(8,128)(2,1)} %shard_map.46) | data formatting | bytes 524288

commit v10 on v5

--- a/solution.py
+++ b/solution.py
@@ -22,10 +22,10 @@
 S_STAT = 18
 S_ATT = 20
 S_FAR = 54
-S_PLAIN = 58
-S_LATER = 62
-S_SIDE = 66
-S_COUNT = 68
+S_PLAIN = 62
+S_LATER = 70
+S_SIDE = 78
+S_COUNT = 80
 
 
 def device_at(x, y, core):
@@ -35,7 +35,7 @@
 def kernel(
     q_hbm, k_hbm, v_hbm, w_hbm, out_ref,
     q_ref, k_ref, q_s, kv, s0, s1, p1, fade1, acc, mrow, o_send, s_send, o_recv, s_recv,
-    att, w, terms, far_in, plain_in, added, added_in, side, side_in, mine, fetched, send, recv,
+    att, w, terms, far_in, plain_in, added, added_in, side, side_in, fetched, send, recv,
 ):
     c, h = lax.axis_index("ctx"), lax.axis_index("head")
     x, y, core = c // 8, (c // 2) % 4, c % 2
@@ -117,10 +117,12 @@
         mrow[r] = jnp.full((ROWS, HD), NEG, jnp.float32)
 
     def place(t):
-        f, q = (t - 8) // 12, (t - 8) % 12
-        pair = jnp.where(t < 8, t // 2 % 2, jnp.where(q < 8, 2 + q // 2, 6 + q % 2))
-        late = jnp.where(q < 8, q % 2, 1 - (q - 8) // 2) * 2 + f
-        row = jnp.where(t < 8, t // 4 * 2 + t % 2, late)
+        q = (t - 8) % 12
+        early = jnp.where(q < 8, 2 + q // 2, 6 + q % 2)
+        early_row = jnp.where(q < 8, q % 2, 1 - (q - 8) // 2) * 2
+        pair = jnp.where(t < 8, t // 2 % 2, jnp.where(t < 20, early, 2 + q % 6))
+        row = jnp.where(t < 8, t // 4 * 2 + t % 2, early_row)
+        row = jnp.where(t < 20, row, (1 - q // 6) * 2 + 1)
         i = pair - 2
         middle = 12 + 2 * (i % 2) + i // 2
         one = jnp.where(pair < 2, 2 * pair, jnp.where(pair < 6, middle, 2 * pair - 4))
@@ -258,86 +260,91 @@
         return copies
 
     cols = w.shape[1] // 2
-    rows = 4 * HALF
+    span = 2 * HALF
 
     def half(i):
         return pl.ds(i * cols, cols)
 
-    def block(distance):
-        return pl.ds(pl.multiple_of(((z + distance) % 4) * rows, rows), rows)
-
-    far_copy = [
-        [
-            remote(terms.at[f, block(2), half(i)], far_in.at[f, i], S_FAR + 2 * f + i, z_ways[i])
-            for i in range(2)
+    def block(distance, g):
+        side_of = e if g == 1 else 1 - e
+        start = (((z + distance) % 4) * 2 + side_of) * span
+        return pl.ds(pl.multiple_of(start, span), span)
+
+    def z_copies(number, source_of, target):
+        return [
+            [
+                [
+                    remote(
+                        source_of(f, g, i), target.at[f, g, i], number + 4 * f + 2 * g + i,
+                        z_ways[i],
+                    )
+                    for i in range(2)
+                ]
+                for g in range(2)
+            ]
+            for f in range(2)
         ]
-        for f in range(2)
-    ]
-    plain_copy = [
-        [
-            remote(
-                terms.at[f, block(1 + 2 * i), half(1 - i)], plain_in.at[f, i],
-                S_PLAIN + 2 * f + i, z_ways[i],
+
+    far_copy = z_copies(S_FAR, lambda f, g, i: terms.at[f, block(2, g), half(i)], far_in)
+    plain_copy = z_copies(
+        S_PLAIN, lambda f, g, i: terms.at[f, block(1 + 2 * i, g), half(1 - i)], plain_in
+    )
+    later_copy = z_copies(S_LATER, lambda f, g, i: added.at[f, g, i], added_in)
+    side_copy = [remote(side.at[f], side_in.at[f], S_SIDE + f, to_side) for f in range(2)]
+
+    def project(f, i):
+        terms[f, :, half(i)] = jnp.dot(
+            att[f], w[:, half(i)], preferred_element_type=jnp.float32
+        ).astype(jnp.bfloat16)
+        for g in range(2):
+            far_copy[f][g][i].start()
+        if i == 1:
+            for j in range(2):
+                plain_copy[f][0][j].start()
+
+    def add_on(f, g):
+        for i in range(2):
+            far_copy[f][g][i].wait_recv()
+            added[f, g, i] = (
+                terms[f, block(1 + 2 * i, g), half(i)].astype(jnp.float32)
+                + far_in[f, g, i].astype(jnp.float32)
+            ).astype(jnp.bfloat16)
+            later_copy[f][g][i].start()
+
+    def reduce_added(f):
+        add_on(f, 0)
+        for i in range(2):
+            plain_copy[f][1][i].start()
+        add_on(f, 1)
+
+    def summed(f, g, i):
+        return (
+            terms[f, block(0, g), half(i)].astype(jnp.float32)
+            + added_in[f, g, i].astype(jnp.float32)
+            + plain_in[f, g, 1 - i].astype(jnp.float32)
+        )
+
+    def wait_sums(f, g):
+        for i in range(2):
+            plain_copy[f][g][i].wait_recv()
+            later_copy[f][g][i].wait_recv()
+
+    def reduce_last(f):
+        wait_sums(f, 0)
+        for i in range(2):
+            side[f, :, half(i)] = summed(f, 0, i).astype(jnp.bfloat16)
+        side_copy[f].start()
+
+    def reduce_end(f):
+        wait_sums(f, 1)
+        side_copy[f].wait_recv()
+        for i in range(2):
+            done = (summed(f, 1, i) + side_in[f, :, half(i)].astype(jnp.float32)).astype(
+                jnp.bfloat16
             )
-            for i in range(2)
-        ]
-        for f in range(2)
-    ]
-    later_copy = [
-        [
-            remote(added.at[f, i], added_in.at[f, i], S_LATER + 2 * f + i, z_ways[i])
-            for i in range(2)
-        ]
-        for f in range(2)
-    ]
-    side_copy = [remote(side.at[f], side_in.at[f], S_SIDE + f, to_side) for f in range(2)]
-
-    def project(f):
-        for i in range(2):
-            terms[f, :, half(i)] = jnp.dot(
-                att[f], w[:, half(i)], preferred_element_type=jnp.float32
-            ).astype(jnp.bfloat16)
-            far_copy[f][i].start()
-        for i in range(2):
-            plain_copy[f][i].start()
-
-    def reduce_added(f):
-        for i in range(2):
-            far_copy[f][i].wait_recv()
-            added[f, i] = (
-                terms[f, block(1 + 2 * i), half(i)].astype(jnp.float32)
-                + far_in[f, i].astype(jnp.float32)
-            ).astype(jnp.bfloat16)
-            later_copy[f][i].start()
-
-    def reduce_last(f):
-        for i in range(2):
-            plain_copy[f][i].wait_recv()
-        for i in range(2):
-            later_copy[f][i].wait_recv()
-
-        def summed(s, i):
-            size = rows // 2
-            part = pl.ds(pl.multiple_of(s * size, size), size)
-            own = pl.ds(pl.multiple_of(z * rows + s * size, size), size)
-            return (
-                terms[f, own, half(i)].astype(jnp.float32)
-                + added_in[f, i, part].astype(jnp.float32)
-                + plain_in[f, 1 - i, part].astype(jnp.float32)
-            )
-
-        for i in range(2):
-            side[f, :, half(i)] = summed(1 - e, i).astype(jnp.bfloat16)
-        side_copy[f].start()
-        for i in range(2):
-            mine[f, :, half(i)] = summed(e, i)
-
-    def reduce_end(f):
-        side_copy[f].wait_recv()
-        done = (mine[f] + side_in[f].astype(jnp.float32)).astype(jnp.bfloat16)
-        for i in range(2):
-            start = i * RUN + f * HALF
-            out_ref[start : start + HALF] = done[i * HALF : (i + 1) * HALF]
+            for k in range(2):
+                start = k * RUN + f * HALF
+                out_ref[start : start + HALF, half(i)] = done[k * HALF : (k + 1) * HALF]
 
     def wait_all(*copies):
         for copy in copies:
@@ -372,9 +379,9 @@
         (11, lambda: combine(0)),
         (11, lambda: gather_own(0)),
         (12, lambda: gather_x(0)),
+        (13, lambda: finish_neighbour(1)),
         (13, lambda: gather_y(0, 0)),
         (14, lambda: gather_y(0, 1)),
-        (15, lambda: finish_neighbour(1)),
         (15, lambda: gather_y2(0, 0)),
     ]
 
@@ -406,29 +413,33 @@
     score(0, s0)
     lax.fori_loop(0, 16, unit, 0)
     add_values(31, p1[...], fade1[...])
+    combine(1)
+    gather_own(1)
     gather_y2(0, 1)
     w_copy.wait()
     gather_end(0)
-    project(0)
-    combine(1)
-    gather_own(1)
+    project(0, 0)
     gather_x(1)
-    reduce_added(0)
     gather_y(1, 0)
+    project(0, 1)
     gather_y(1, 1)
     gather_y2(1, 0)
-    reduce_last(0)
+    reduce_added(0)
     gather_y2(1, 1)
     gather_end(1)
-    project(1)
+    project(1, 0)
+    project(1, 1)
+    reduce_last(0)
+    reduce_added(1)
     reduce_end(0)
-    reduce_added(1)
     reduce_last(1)
     reduce_end(1)
 
     sent += side_copy
     for f in range(2):
-        sent += gather_sent(f) + far_copy[f] + plain_copy[f] + later_copy[f]
+        sent += gather_sent(f)
+        for copies in far_copy[f] + plain_copy[f] + later_copy[f]:
+            sent += copies
     for copy in sent:
         copy.wait_send()
 
@@ -439,7 +450,7 @@
     all_rows = tokens // 2 * lax.axis_size("ctx")
     vmem, anywhere = pl.BlockSpec(memory_space=pltpu.VMEM), pl.BlockSpec(memory_space=pl.ANY)
     bf16, f32 = jnp.bfloat16, jnp.float32
-    piece = pltpu.VMEM((2, 2, 2 * tokens, cols // 2), bf16)
+    piece = pltpu.VMEM((2, 2, 2, tokens, cols // 2), bf16)
     return pl.pallas_call(
         kernel,
         out_shape=jax.ShapeDtypeStruct((2 * tokens, cols), bf16),
@@ -469,7 +480,6 @@
             piece,
             pltpu.VMEM((2, tokens, cols), bf16),
             pltpu.VMEM((2, tokens, cols), bf16),
-            pltpu.VMEM((2, tokens, cols), f32),
             pltpu.SemaphoreType.DMA((5,)),
             pltpu.SemaphoreType.DMA((S_COUNT,)),
             pltpu.SemaphoreType.DMA((S_COUNT,)),

time: 90.2 us -> 82.9 us (0.919)
  Pallas kernels: 87.9 us -> 80.5 us
    pallas_call x1, Pallas kernels: 87.9 us -> 80.5 us  [body(): pl.pallas_call(kernel, out_shape=jax.ShapeDtypeStruct((2 * tokens, cols),...]
where the time goes in v10:
time: 82.9 us; the launch traced here: 82.1 us
  Pallas kernels  80.5 us (97%)
  local copies, waits for them, and re-layouts  1.67 us (2%)
    pallas_call x1, Pallas kernels, body(): pl.pallas_call(kernel, out_shape=jax.ShapeDtypeStruct((2 * tokens, cols),...  80.5 us
    unnamed x1, local copies, waits for them, and re-layouts  1.67 us

profile of v10, /device:TPU:0, one launch (start us, length us, event | category | flops | bytes accessed | tf_op | source)
XLA Modules:
  0.0 82.1 jit_solution(12970102902160715931)
XLA Ops:
  0.0 80.5 %shard_map.46 = bf16[128,1024]{1,0:T(8,128)(2,1)} custom-call(bf16[64,2048]{1,0:T(8,128)(2,1)} %q_hbm.1, bf16[1024,128]{1,0:T(8,128)(2,1)} %k_hbm.1, bf16[1024,128]{1,0:T(8,128)(2,1)} %v_hbm.1, bf16[2048,1024]{1,0:T(8,128)(2,1)} %w_hbm.1), custom_call_target="tpu_custom_call" | custom-call | flops 12999999488 | bytes 5000000 | tf_op jit(solution)/shard_map/pallas_call | solution.py:454
  80.5 1.7 %copy.6 = bf16[128,1024]{1,0:T(8,128)(2,1)} copy(bf16[128,1024]{1,0:T(8,128)(2,1)} %shard_map.46) | data formatting | bytes 524288

commit v11 on v10

--- a/solution.py
+++ b/solution.py
@@ -13,7 +13,7 @@
 ROWS = 512
 HALF = 32
 KEYS = 512
-LOG2E = math.log2(math.e)
+
 MESH = pl.DeviceIdType.MESH
 
 S_KV = 0
@@ -40,7 +40,7 @@
     c, h = lax.axis_index("ctx"), lax.axis_index("head")
     x, y, core = c // 8, (c // 2) % 4, c % 2
     z, e = h // 2, h % 2
-    scale = LOG2E / math.sqrt(HD)
+    scale = 1.0 / math.sqrt(HD)
 
     to_core = (device_at(x, y, 1 - core), h)
     to_up = (device_at(x, (y + 1) % 4, core), h)
@@ -158,9 +158,9 @@
         scores = jnp.concatenate(pieces, axis=1)
         old = mrow[row]
         new = jnp.maximum(old, jnp.max(scores, axis=1, keepdims=True))
-        weights = jnp.exp2(scores - jnp.concatenate([new] * (2 * KEYS // HD), axis=1))
+        weights = jnp.exp(scores - jnp.concatenate([new] * (2 * KEYS // HD), axis=1))
         mrow[row] = new
-        return weights.astype(jnp.bfloat16), jnp.exp2(old - new)
+        return weights.astype(jnp.bfloat16), jnp.exp(old - new)
 
     def add_values(t, weights, fade):
         one, two, row = place(t)
@@ -174,7 +174,7 @@
 
     def normalised(row):
         total = acc[row, :, HD : 2 * HD]
-        return acc[row, :, 0:HD] / total, mrow[row] + jnp.log(total) * LOG2E
+        return acc[row, :, 0:HD] / total, mrow[row] + jnp.log(total)
 
     def finish_neighbour(f):
         value, level = normalised(2 + f)
@@ -193,7 +193,7 @@
         s_copy[f].wait_recv()
         other = jnp.broadcast_to(s_recv[f, 0:1], (HD, ROWS)).T
         top = jnp.maximum(level, other)
-        part_a, part_b = jnp.exp2(level - top), jnp.exp2(other - top)
+        part_a, part_b = jnp.exp(level - top), jnp.exp(other - top)
         done = (value * part_a + o_recv[f].astype(jnp.float32) * part_b) / (part_a + part_b)
         done = done.astype(jnp.bfloat16)
         for i in range(16):

time: 82.9 us -> 83.3 us (level)
  no operation moved by 1% of the time
where the time goes in v11:
time: 83.3 us; the launch traced here: 82.6 us
  Pallas kernels  80.9 us (97%)
  local copies, waits for them, and re-layouts  1.67 us (2%)
    pallas_call x1, Pallas kernels, body(): pl.pallas_call(kernel, out_shape=jax.ShapeDtypeStruct((2 * tokens, cols),...  80.9 us
    unnamed x1, local copies, waits for them, and re-layouts  1.67 us

profile of v11, /device:TPU:0, one launch (start us, length us, event | category | flops | bytes accessed | tf_op | source)
XLA Modules:
  0.0 82.6 jit_solution(5818864092624871619)
XLA Ops:
  0.0 80.9 %shard_map.46 = bf16[128,1024]{1,0:T(8,128)(2,1)} custom-call(bf16[64,2048]{1,0:T(8,128)(2,1)} %q_hbm.1, bf16[1024,128]{1,0:T(8,128)(2,1)} %k_hbm.1, bf16[1024,128]{1,0:T(8,128)(2,1)} %v_hbm.1, bf16[2048,1024]{1,0:T(8,128)(2,1)} %w_hbm.1), custom_call_target="tpu_custom_call" | custom-call | flops 12999999488 | bytes 5000000 | tf_op jit(solution)/shard_map/pallas_call | solution.py:454
  80.9 1.7 %copy.6 = bf16[128,1024]{1,0:T(8,128)(2,1)} copy(bf16[128,1024]{1,0:T(8,128)(2,1)} %shard_map.46) | data formatting | bytes 524288

commit v12 on v10

--- a/solution.py
+++ b/solution.py
@@ -244,8 +244,8 @@
         arrived(f, 15 + plane, plane, 2, 1)
         gather_start(f, 4 * plane + 2, plane, 2, to_core)
 
-    def gather_end(f):
-        for plane in range(2):
+    def gather_end(f, planes=(0, 1)):
+        for plane in planes:
             for dy in range(4):
                 arrived(f, 4 * plane + dy, plane, dy, None, 1 - core)
 
@@ -292,10 +292,20 @@
     later_copy = z_copies(S_LATER, lambda f, g, i: added.at[f, g, i], added_in)
     side_copy = [remote(side.at[f], side_in.at[f], S_SIDE + f, to_side) for f in range(2)]
 
+    def project_plane(f, plane, i):
+        size = att.shape[1] // 2
+        rows = pl.ds(pl.multiple_of((1 - x if plane else x) * size, size), size)
+        terms[f, rows, half(i)] = jnp.dot(
+            att[f, rows], w[:, half(i)], preferred_element_type=jnp.float32
+        ).astype(jnp.bfloat16)
+
     def project(f, i):
         terms[f, :, half(i)] = jnp.dot(
             att[f], w[:, half(i)], preferred_element_type=jnp.float32
         ).astype(jnp.bfloat16)
+        send_products(f, i)
+
+    def send_products(f, i):
         for g in range(2):
             far_copy[f][g][i].start()
         if i == 1:
@@ -425,10 +435,14 @@
     gather_y(1, 1)
     gather_y2(1, 0)
     reduce_added(0)
+    gather_end(1, (0,))
+    project_plane(1, 0, 0)
     gather_y2(1, 1)
-    gather_end(1)
-    project(1, 0)
-    project(1, 1)
+    project_plane(1, 0, 1)
+    gather_end(1, (1,))
+    for i in range(2):
+        project_plane(1, 1, i)
+        send_products(1, i)
     reduce_last(0)
     reduce_added(1)
     reduce_end(0)

time: 82.9 us -> 82.8 us (level)
  no operation moved by 1% of the time
where the time goes in v12:
time: 82.8 us; the launch traced here: 82.1 us
  Pallas kernels  80.4 us (97%)
  local copies, waits for them, and re-layouts  1.67 us (2%)
    pallas_call x1, Pallas kernels, body(): pl.pallas_call(kernel, out_shape=jax.ShapeDtypeStruct((2 * tokens, cols),...  80.4 us
    unnamed x1, local copies, waits for them, and re-layouts  1.67 us

profile of v12, /device:TPU:0, one launch (start us, length us, event | category | flops | bytes accessed | tf_op | source)
XLA Modules:
  0.0 82.1 jit_solution(12389630386785546203)
XLA Ops:
  0.0 80.4 %shard_map.46 = bf16[128,1024]{1,0:T(8,128)(2,1)} custom-call(bf16[64,2048]{1,0:T(8,128)(2,1)} %q_hbm.1, bf16[1024,128]{1,0:T(8,128)(2,1)} %k_hbm.1, bf16[1024,128]{1,0:T(8,128)(2,1)} %v_hbm.1, bf16[2048,1024]{1,0:T(8,128)(2,1)} %w_hbm.1), custom_call_target="tpu_custom_call" | custom-call | flops 12999999488 | bytes 5000000 | tf_op jit(solution)/shard_map/pallas_call | solution.py:468
  80.4 1.7 %copy.6 = bf16[128,1024]{1,0:T(8,128)(2,1)} copy(bf16[128,1024]{1,0:T(8,128)(2,1)} %shard_map.46) | data formatting | bytes 524288

commit v13 on v12

--- a/solution.py
+++ b/solution.py
@@ -106,12 +106,14 @@
     o_copy = [remote(o_send.at[f], o_recv.at[f], S_O + f, to_x) for f in range(2)]
     s_copy = [remote(s_send.at[f], s_recv.at[f], S_STAT + f, to_x) for f in range(2)]
 
+    own_up[0].start()
+    own_down[0].start()
+    q_copy[0].start()
     for i in range(2):
         own_core[i].start()
-    q_copy[0].start()
-    own_up[0].start()
-    own_down[0].start()
     q_copy[1].start()
+    own_up[1].start()
+    own_down[1].start()
     for r in range(4):
         acc[r] = jnp.zeros((ROWS, 2 * HD), jnp.float32)
         mrow[r] = jnp.full((ROWS, HD), NEG, jnp.float32)
@@ -367,8 +369,6 @@
 
     def start_rest():
         wait_all(*own_core)
-        own_up[1].start()
-        own_down[1].start()
 
     before = [
         (0, start_rest),

time: 82.8 us -> 82.8 us (level)
  no operation moved by 1% of the time
where the time goes in v13:
time: 82.8 us; the launch traced here: 82.1 us
  Pallas kernels  80.4 us (97%)
  local copies, waits for them, and re-layouts  1.67 us (2%)
    pallas_call x1, Pallas kernels, body(): pl.pallas_call(kernel, out_shape=jax.ShapeDtypeStruct((2 * tokens, cols),...  80.4 us
    unnamed x1, local copies, waits for them, and re-layouts  1.67 us

profile of v13, /device:TPU:0, one launch (start us, length us, event | category | flops | bytes accessed | tf_op | source)
XLA Modules:
  0.0 82.1 jit_solution(4530080818868162159)
XLA Ops:
  0.0 80.4 %shard_map.46 = bf16[128,1024]{1,0:T(8,128)(2,1)} custom-call(bf16[64,2048]{1,0:T(8,128)(2,1)} %q_hbm.1, bf16[1024,128]{1,0:T(8,128)(2,1)} %k_hbm.1, bf16[1024,128]{1,0:T(8,128)(2,1)} %v_hbm.1, bf16[2048,1024]{1,0:T(8,128)(2,1)} %w_hbm.1), custom_call_target="tpu_custom_call" | custom-call | flops 12999999488 | bytes 5000000 | tf_op jit(solution)/shard_map/pallas_call | solution.py:468
  80.4 1.7 %copy.6 = bf16[128,1024]{1,0:T(8,128)(2,1)} copy(bf16[128,1024]{1,0:T(8,128)(2,1)} %shard_map.46) | data formatting | bytes 524288
